TPU v7x, 512 devices: a whole 4x8x8 slice. The times are simulated.
512 devices in a mesh: py: 16 (over y, core), pz: 32 (over z, x).
Axes of the slice: x: 4, y: 8, z: 8, core: 2. Of those that a mesh axis runs over, the one named last changes fastest.
Arguments:
- nodal: bfloat16 [16, 14336, 3, 512], P('py', 'pz'), may hold values from -6 to 6
- element_counts: int32 [16, 32], P('py', 'pz'), may hold values from 64 to 448, as said below
- send_slots: int32 [16, 14336], P('py', 'pz'), may hold values from 0 to 511, as said below
- arrival_slots: int32 [16, 16384], P('py', 'pz'), may hold values from 0 to 256, as said below
Outputs:
- spectra: float32 [3, 2, 160, 512, 256], P(None, None, 'py', 'pz')
Inputs may be any that keep to these rules, and one draw needn't show every extreme that they name: `element_counts`: within one index of py the counts sum to 8192; some rank of each index of py holds exactly 448 live slots. `send_slots`: the live positions of one rank are distinct; at most 16 of them fall in any one pencil block's range of 16 positions, and in every draw some rank fills a block's range; positions of slots past the count are arbitrary. `arrival_slots`: the value 256 marks a slot that carries nothing, exactly the slots that no live element of the sending rank names; every local index below 256 appears exactly once in each pencil block.
All inputs are finite; a program needn't handle non-finite values.
Results may differ from a plain program's by a relative error of at most 0.0065.
Values may be sent and summed in bfloat16 or wider, within the bound.
A program may use at most 64 MiB of HBM per device.

v0:
```python
import math

import jax
import jax.numpy as jnp
import numpy as np
from jax import lax
from jax.sharding import PartitionSpec as P

NODE = 8
EX = 64
KX = 160
YE = 2
LZ = 2
AVG = 256


def lobatto_points(number):
    degree = number - 1
    points = np.cos(np.pi * np.arange(number) / degree)
    for sweeps in range(60):
        older_poly = np.ones(number)
        newer_poly = points.copy()
        for degree_now in range(2, degree + 1):
            older_poly, newer_poly = (
                newer_poly,
                ((2 * degree_now - 1) * points * newer_poly - (degree_now - 1) * older_poly)
                / degree_now,
            )
        points = points - (points * newer_poly - older_poly) / (number * newer_poly)
    return np.sort(points)


def vandermonde(number):
    gauss_points = lobatto_points(number)
    uniform = -1.0 + (2.0 * np.arange(number) + 1.0) / number
    columns_list = []
    for column in range(number):
        same = np.arange(number) == column
        numer = np.where(same[None, :], 1.0, uniform[:, None] - gauss_points[None, :])
        denom = np.where(same, 1.0, gauss_points[column] - gauss_points)
        columns_list.append(np.prod(numer / denom[None, :], axis=1))
    return np.stack(columns_list, axis=1)


def evaluate_rounded(coeffs):
    lagrange = vandermonde(NODE)
    operator = jnp.asarray(np.kron(np.kron(lagrange, lagrange), lagrange).T, dtype=jnp.float32)
    upper_part = operator.astype(jnp.bfloat16)
    lower_part = (operator - upper_part.astype(jnp.float32)).astype(jnp.bfloat16)
    flat_rows = coeffs.reshape(-1, coeffs.shape[-1])
    result = jnp.dot(flat_rows, upper_part, preferred_element_type=jnp.float32)
    result = result + jnp.dot(flat_rows, lower_part, preferred_element_type=jnp.float32)
    return result.reshape(coeffs.shape).astype(jnp.bfloat16)


def fourier_tables(mode_count, blocks, node_count):
    length = blocks * node_count
    wavenumber = jnp.arange(mode_count, dtype=jnp.int32)[:, None]
    position = jnp.arange(length, dtype=jnp.int32)[None, :]
    angles = (wavenumber * position % length).astype(jnp.float32) * (2.0 * math.pi / length)
    factor = 1.0 / math.sqrt(length)
    precise = (jnp.stack([jnp.cos(angles), -jnp.sin(angles)]) * factor).reshape(
        2 * mode_count, length
    )
    upper_part = precise.astype(jnp.bfloat16)
    lower_part = (precise - upper_part.astype(jnp.float32)).astype(jnp.bfloat16)
    return (upper_part, lower_part)


def on_device(nodal, element_counts, send_slots, arrival_slots):
    peers = lax.axis_size("pz")
    capacity = nodal.shape[1]
    total_slots = arrival_slots.shape[1]
    slot_count = total_slots // peers
    nodes_all = nodal.shape[3]
    live = jnp.arange(capacity, dtype=jnp.int32) < element_counts[0, 0]
    target = jnp.where(live, send_slots[0], total_slots)
    source_of = jnp.full((total_slots,), capacity, jnp.int32)
    source_of = source_of.at[target].set(jnp.arange(capacity, dtype=jnp.int32), mode="drop")
    values = evaluate_rounded(nodal[0])
    outgoing = jnp.take(values, source_of, axis=0, mode="fill", fill_value=0)
    outgoing = outgoing.reshape(peers, slot_count, 3, nodes_all)
    arrived = lax.all_to_all(outgoing, "pz", split_axis=0, concat_axis=0, tiled=True)
    arrived_rows = arrived.reshape(total_slots, 3, nodes_all)
    slot_of = jnp.zeros((AVG,), jnp.int32)
    slot_of = slot_of.at[arrival_slots[0]].set(
        jnp.arange(total_slots, dtype=jnp.int32), mode="drop"
    )
    placed = jnp.take(arrived_rows, slot_of, axis=0)
    shaped = placed.reshape(LZ, YE, EX, 3, NODE, NODE, NODE)
    columns = shaped.transpose(3, 2, 6, 0, 4, 1, 5).reshape(3, EX * NODE, LZ * NODE * YE * NODE)
    table_upper, table_lower = fourier_tables(KX, EX, NODE)
    spectra = jnp.einsum("rx,cxm->crm", table_upper, columns, preferred_element_type=jnp.float32)
    spectra = spectra + jnp.einsum(
        "rx,cxm->crm", table_lower, columns, preferred_element_type=jnp.float32
    )
    spectra = spectra.reshape(3, 2, KX, LZ * NODE, YE * NODE)
    return lax.all_to_all(spectra, "py", split_axis=2, concat_axis=4, tiled=True)


def solution(mesh):
    placed = (P("py", "pz", None, None), P("py", "pz"), P("py", "pz"), P("py", "pz"))
    return jax.shard_map(
        on_device,
        mesh=mesh,
        in_specs=placed,
        out_specs=P(None, None, "py", "pz", None),
        check_vma=False,
    )
```

profile of v0, /device:TPU:1, one launch (start us, length us, event | category | flops | bytes accessed | tf_op | source)
XLA Modules:
  0.0 185.0 jit_solution(2625613212948167545)
XLA Ops:
  0.7 0.7 compare_select_fusion
  1.3 2.9 %scatter_custom_fusion.1 = s32[512]{0:T(512)S(1)} fusion(s32[448]{0:T(512)S(1)} %bitcast.54, s32[448]{0:T(512)S(1)} %iota.32, s32[]{:T(128)} %constant.50.clone.1), kind=kCustom, calls=%fused_computation.35 | custom fusion | bytes 2052 | tf_op jit(solution)/shard_map/scatter | solution.py:79
  4.4 2.5 %copy.39 = bf16[1,448,3,512]{3,2,1,0:T(4,128)(2,1)S(1)} copy(bf16[1,448,3,512]{3,1,2,0:T(8,128)(2,1)} %param.5) | data formatting | bytes 2752512 | tf_op args[0]
  6.9 1.2 reshape_squeeze.3
  8.1 2.0 %fusion.17 = f32[512,1344]{0,1:T(8,128)S(1)} fusion(bf16[1344,512]{1,0:T(8,128)(2,1)S(1)} %reshape_squeeze.3, bf16[512,512]{1,0:T(8,128)(2,1)} %constant.61), kind=kOutput, calls=%fused_computation.40 | convolution fusion | flops 704643072 | bytes 4653056 | tf_op jit(solution)/shard_map/dot_general | solution.py:51
  10.1 0.9 fusion.1
  11.0 0.8 convert_element_type.76
  11.9 3.8 %gather_fusion = bf16[512,3,512]{2,1,0:T(4,128)(2,1)} fusion(bf16[448,3,512]{2,1,0:T(4,128)(2,1)S(1)} %convert_element_type.76, s32[1024]{0:T(1024)S(1)} %pad_clamp_fusion.1), kind=kCustom, calls=%fused_computation | custom fusion | bytes 3147776 | tf_op jit(solution)/shard_map/jit(_take)/gather | solution.py:81
  15.7 3.2 %copy_select_fusion = bf16[32,16,3,512]{3,1,2,0:T(8,128)(2,1)} fusion(bf16[32,16,3,512]{3,2,1,0:T(4,128)(2,1)} %bitcast.50, pred[32,16]{1,0:T(8,128)(4,1)S(1)} %broadcast_in_dim.47), kind=kLoop, calls=%fused_computation.9 | loop fusion | flops 786432 | bytes 3146240 | tf_op jit(solution)/shard_map/jit(_take)/select_n | solution.py:81
  18.9 13.8 %all-to-all-start = ((bf16[32,16,3,512]{3,1,2,0:T(8,128)(2,1)}), bf16[32,16,3,512]{3,1,2,0:T(8,128)(2,1)S(1)}, u32[]{:S(2)}, u32[]{:S(2)}) async-start(bf16[32,16,3,512]{3,1,2,0:T(8,128)(2,1)} %copy_select_fusion), calls=%async_computation | async-start | bytes 3145728 | tf_op jit(solution)/shard_map/all_to_all | solution.py:83
  32.7 2.6 %scatter_custom_fusion = s32[256]{0:T(256)S(1)} fusion(s32[512]{0:T(512)S(1)} %bitcast.55, s32[512]{0:T(512)S(1)} %iota.30, s32[]{:T(128)} %constant.27.clone.1), kind=kCustom, calls=%fused_computation.37 | custom fusion | bytes 1028 | tf_op jit(solution)/shard_map/scatter | solution.py:86
  35.5 1.3 sine_negate_fusion
  36.8 0.8 subtract_convert_fusion
  37.6 33.0 %all-to-all-done = bf16[32,16,3,512]{3,1,2,0:T(8,128)(2,1)S(1)} async-done(((bf16[32,16,3,512]{3,1,2,0:T(8,128)(2,1)}), bf16[32,16,3,512]{3,1,2,0:T(8,128)(2,1)S(1)}, u32[]{:S(2)}, u32[]{:S(2)}) %all-to-all-start) | async-done | bytes 1572896 | tf_op jit(solution)/shard_map/all_to_all | solution.py:83
  70.6 2.8 %copy.41 = bf16[32,16,3,512]{3,2,1,0:T(4,128)(2,1)} copy(bf16[32,16,3,512]{3,1,2,0:T(8,128)(2,1)S(1)} %all-to-all-done) | data formatting | bytes 3145728 | tf_op jit(solution)/shard_map/all_to_all | solution.py:83
  73.4 3.1 %gather_fusion.1 = bf16[256,3,512]{2,1,0:T(4,128)(2,1)S(1)} fusion(bf16[512,3,512]{2,1,0:T(4,128)(2,1)} %bitcast.51, s32[1024]{0:T(1024)S(1)} %pad_clamp_fusion), kind=kCustom, calls=%fused_computation.1 | custom fusion | bytes 1573888 | tf_op jit(solution)/shard_map/jit(_take)/gather | solution.py:89
  76.5 0.7 copy.42
  77.3 0.7 gather.15
  77.9 1.4 fusion.2
  79.3 9.2 %copy.43 = bf16[3,64,8,2,8,2,8]{2,1,6,5,4,3,0:T(8,128)(2,1)} copy(bf16[3,64,8,2,8,2,8]{1,5,3,2,6,4,0:T(2,128)(2,1)S(1)} %fusion.2) | data formatting | bytes 1572864 | tf_op jit(solution)/shard_map/transpose | solution.py:91
  88.6 18.8 %reshape.171 = bf16[3,512,256]{1,2,0:T(8,128)(2,1)S(1)} reshape(bf16[3,64,8,2,8,2,8]{2,1,6,5,4,3,0:T(8,128)(2,1)} %copy.43) | data formatting | bytes 1572864 | tf_op jit(solution)/shard_map/reshape | solution.py:91
  107.8 1.4 fusion.3
  109.2 1.6 copy.46
  110.8 1.3 reshape.172
  112.1 5.8 %copy.47 = f32[3,2,160,16,16]{4,3,1,0,2:T(8,128)} copy(f32[3,2,160,16,16]{2,1,4,3,0:T(2,128)S(1)} %reshape.172) | data formatting | bytes 1966080 | tf_op jit(solution)/shard_map/reshape | solution.py:97
  117.8 5.4 %reshape.213 = f32[16,1,15360]{2,1,0:T(1,128)S(1)} reshape(f32[160,3,2,16,16]{4,3,2,1,0:T(8,128)} %bitcast.48) | data formatting | bytes 1966080
  123.2 36.3 %all_to_all.23 = f32[16,1,15360]{2,1,0:T(1,128)S(1)} all-to-all(f32[16,1,15360]{2,1,0:T(1,128)S(1)} %reshape.213), channel_id=1, replica_groups=mesh['py'=16,'pz'=32] {'py'}, dimensions={0} | all-to-all | bytes 1966080 | tf_op jit(solution)/shard_map/all_to_all | solution.py:98
  159.5 0.5 broadcast.159
  160.0 3.0 %reduce = f32[16,15360]{1,0:T(8,128)S(1)} reduce(f32[16,1,15360]{2,1,0:T(1,128)S(1)} %all_to_all.23, f32[]{:T(128)} %broadcast.159), dimensions={1}, to_apply=%all_to_all.17.reduce_sub_computation | reduce | bytes 1966084 | tf_op jit(solution)/shard_map/all_to_all | solution.py:98
  163.0 4.6 %reshape.214 = f32[160,3,2,16,16]{4,3,2,1,0:T(8,128)} reshape(f32[16,15360]{1,0:T(8,128)S(1)} %reduce) | data formatting | bytes 1966080
  167.5 10.9 %copy.49 = f32[3,2,10,16,16,16]{5,4,3,2,1,0:T(8,128)} copy(f32[3,2,10,16,16,16]{5,3,1,0,2,4:T(8,128)} %bitcast.49) | data formatting | bytes 1966080 | tf_op jit(solution)/shard_map/all_to_all | solution.py:98
  178.5 6.5 %all_to_all.20 = f32[3,2,10,16,256]{4,3,2,1,0:T(8,128)} reshape(f32[3,2,10,16,16,16]{5,4,3,2,1,0:T(8,128)} %copy.49) | data formatting | bytes 1966080 | tf_op jit(solution)/shard_map/all_to_all | solution.py:98
  (18 shorter events, 0.7 us)
Async XLA Ops:
  8.1 2.0 %copy-start.1 = (bf16[512,512]{1,0:T(8,128)(2,1)S(1)}, bf16[512,512]{1,0:T(8,128)(2,1)}, u32[]{:S(2)}) copy-start(bf16[512,512]{1,0:T(8,128)(2,1)} %constant.64) | copy-start | bytes 1572868
  18.9 13.9 %copy-start.2 = (s32[1,512]{1,0:T(1,128)S(1)}, s32[1,512]{1,0:T(1,128)}, u32[]{:S(2)}) copy-start(s32[1,512]{1,0:T(1,128)} %param.8) | copy-start | bytes 6148
  18.9 51.7 %all-to-all-start = ((bf16[32,16,3,512]{3,1,2,0:T(8,128)(2,1)}), bf16[32,16,3,512]{3,1,2,0:T(8,128)(2,1)S(1)}, u32[]{:S(2)}, u32[]{:S(2)}) async-start(bf16[32,16,3,512]{3,1,2,0:T(8,128)(2,1)} %copy_select_fusion), calls=%async_computation | async-start | bytes 3145728 | tf_op jit(solution)/shard_map/all_to_all | solution.py:83
  88.6 18.8 %copy-start = (bf16[2,160,512]{2,1,0:T(8,128)(2,1)S(1)}, bf16[2,160,512]{2,1,0:T(8,128)(2,1)}, u32[]{:S(2)}) copy-start(bf16[2,160,512]{2,1,0:T(8,128)(2,1)} %get-tuple-element.6) | copy-start | bytes 983044
where the time goes:
time: 186 us; the launch traced here: 185 us
  local copies, waits for them, and re-layouts  86 us (46%)
  blocking collectives  36.3 us (20%)
  waiting for transfers between devices  33 us (18%)
  starting transfers between devices  13.8 us (7%)
  other arithmetic  10.3 us (6%)
  matrix products  4.72 us (3%)
    all_to_all x1, blocking collectives, on_device(): lax.all_to_all(spectra, 'py', split_axis=2, concat_axis=4, tiled=True)  36.3 us
    all_to_all x1, waiting for transfers between devices, on_device(): lax.all_to_all(outgoing, 'pz', split_axis=0, concat_axis=0, tiled=True)  33 us
    reshape x1, local copies, waits for them, and re-layouts, on_device(): shaped.transpose(3, 2, 6, 0, 4, 1, 5)  18.8 us
    all_to_all x3, local copies, waits for them, and re-layouts, on_device(): lax.all_to_all(spectra, 'py', split_axis=2, concat_axis=4, tiled=True)  18 us
    all_to_all x1, starting transfers between devices, on_device(): lax.all_to_all(outgoing, 'pz', split_axis=0, concat_axis=0, tiled=True)  13.8 us
    unnamed x9, local copies, waits for them, and re-layouts  12.5 us
    transpose x1, local copies, waits for them, and re-layouts, on_device(): shaped.transpose(3, 2, 6, 0, 4, 1, 5)  9.25 us
    reshape x2, local copies, waits for them, and re-layouts, on_device(): spectra = spectra.reshape(3, 2, KX, LZ * NODE, YE * NODE)  7.05 us
  transfers between devices with their start and end apart: 1, of which 1 were waited for; matrix products, arithmetic and copies ran while one was open for 3% of the time, Pallas kernels for 0%

commit v1 on v0

v1 whole, which is shorter than its diff:
```python
import functools
import math

import jax
import jax.numpy as jnp
import ml_dtypes
import numpy as np
from jax import lax
from jax.experimental import pallas as pl
from jax.experimental.pallas import tpu as pltpu
from jax.sharding import PartitionSpec as P

NODE = 8
YE = 2
LZ = 2
BLOCKS = YE * LZ
COMPONENTS = 3
SLOTS = 16
X_RING = 4
MODES = 10
USED = 2 * MODES
PADDED = 32
GROUP = 4
BF16 = jnp.bfloat16
F32 = jnp.float32
MESH = pl.DeviceIdType.MESH


def lobatto_points(number):
    degree = number - 1
    points = np.cos(np.pi * np.arange(number) / degree)
    for sweeps in range(60):
        older_poly = np.ones(number)
        newer_poly = points.copy()
        for degree_now in range(2, degree + 1):
            older_poly, newer_poly = (
                newer_poly,
                ((2 * degree_now - 1) * points * newer_poly - (degree_now - 1) * older_poly)
                / degree_now,
            )
        points = points - (points * newer_poly - older_poly) / (number * newer_poly)
    return np.sort(points)


def vandermonde(number):
    gauss_points = lobatto_points(number)
    uniform = -1.0 + (2.0 * np.arange(number) + 1.0) / number
    columns_list = []
    for column in range(number):
        same = np.arange(number) == column
        numer = np.where(same[None, :], 1.0, uniform[:, None] - gauss_points[None, :])
        denom = np.where(same, 1.0, gauss_points[column] - gauss_points)
        columns_list.append(np.prod(numer / denom[None, :], axis=1))
    return np.stack(columns_list, axis=1)


def fourier_table(bands, elements):
    length = elements * NODE
    wavenumber = np.arange(bands * MODES)[:, None]
    angles = (wavenumber * np.arange(length)[None, :] % length) * (2.0 * np.pi / length)
    dft = np.stack([np.cos(angles), -np.sin(angles)]) / math.sqrt(length)
    dft = dft.reshape(2, bands, MODES, elements, NODE)
    nodes = np.einsum("tikeh,hn->itken", dft, vandermonde(NODE))
    nodes = nodes.reshape(bands, USED, elements, NODE // 2, 2).transpose(4, 0, 1, 3, 2)
    table = np.zeros((2, bands, PADDED, NODE // 2, elements))
    table[:, :, :USED] = nodes
    return table.reshape(2, bands * PADDED, NODE // 2 * elements).astype(ml_dtypes.bfloat16)


def plane_table():
    lagrange = vandermonde(NODE)
    eye = np.eye(2)
    table = np.einsum("ac,bd,q,fu,gv->abquvcfdg", eye, eye, np.ones(2), lagrange, lagrange)
    return table.reshape(BLOCKS * 128, 256).astype(ml_dtypes.bfloat16)


def transfer_kernel(
    n_py, n_pz, nodal, counts, send_slots, arrival_slots, fourier, plane, received,
    nodes, fourier_here, plane_here, pick, place, order, outgoing, arrived, stacked, coeffs,
    load_sem, send_sem, arrive_sem, spread_sem, receive_sem,
):
    me_y = lax.axis_index("py")
    me_z = lax.axis_index("pz")
    z_ring = n_pz // X_RING
    my_plane, my_column = me_z // X_RING, me_z % X_RING
    capacity = nodes.shape[1]
    values = nodes.shape[2]
    elements = place.shape[0] // BLOCKS
    total_slots = n_pz * SLOTS

    barrier = pltpu.get_barrier_semaphore()

    def greet_z(step, carry):
        pl.semaphore_signal(
            barrier, inc=1, device_id={"pz": (me_z + step) % n_pz}, device_id_type=MESH
        )
        return carry

    def greet_y(step, carry):
        pl.semaphore_signal(
            barrier, inc=1, device_id={"py": (me_y + step) % n_py}, device_id_type=MESH
        )
        return carry

    lax.fori_loop(1, n_pz, greet_z, 0)
    lax.fori_loop(1, n_py, greet_y, 0)

    loads = [
        pltpu.make_async_copy(nodal.at[c], nodes.at[c], load_sem.at[c]) for c in range(COMPONENTS)
    ]
    loads.append(pltpu.make_async_copy(fourier, fourier_here, load_sem.at[COMPONENTS]))
    loads.append(pltpu.make_async_copy(plane, plane_here, load_sem.at[COMPONENTS + 1]))
    for load in loads:
        load.start()

    column = lax.broadcasted_iota(jnp.int32, (1, capacity), 1)
    target = jnp.where(column < counts[...], send_slots[...], -1)
    row = lax.broadcasted_iota(jnp.int32, (total_slots, capacity), 0)
    pick[...] = jnp.where(row == target, 1.0, 0.0).astype(BF16)
    old = lax.broadcasted_iota(jnp.int32, (values, values), 0)
    new = lax.broadcasted_iota(jnp.int32, (values, values), 1)
    wanted = (new % 64) * NODE + new // 64
    order[...] = jnp.where(old == wanted, 1.0, 0.0).astype(BF16)

    def pack(c):
        loads[c].wait()
        turned = jnp.dot(nodes[c], order[...], preferred_element_type=F32).astype(BF16)
        packed = jnp.dot(pick[...], turned, preferred_element_type=F32).astype(BF16)
        outgoing[c] = packed.reshape(n_pz, SLOTS, values)

    def send_to(c, plane_step, column_step):
        peer_plane = (my_plane + plane_step + z_ring) % z_ring
        peer = peer_plane * X_RING + (my_column + column_step) % X_RING
        pltpu.make_async_remote_copy(
            src_ref=outgoing.at[c, peer],
            dst_ref=arrived.at[c, me_z],
            send_sem=send_sem.at[c],
            recv_sem=arrive_sem.at[c],
            device_id={"pz": peer},
            device_id_type=MESH,
        ).start()

    def send(c):
        def far(step, carry):
            turn = step // X_RING
            send_to(c, (turn + 2) // 2 * (1 - 2 * (turn % 2)), step % X_RING)
            return carry

        def near(step, carry):
            send_to(c, 0, step)
            return carry

        lax.fori_loop(0, (z_ring - 1) * X_RING, far, 0)
        lax.fori_loop(1, X_RING, near, 0)
        arrived[c, me_z] = outgoing[c, me_z]

    def wait_for(ref, blocks, sem):
        part = ref.at[pl.ds(0, blocks)]
        pltpu.make_async_copy(part, part, sem).wait()

    rows = GROUP * PADDED
    groups = n_py // GROUP

    def transform(c):
        wait_for(arrived.at[c], n_pz - 1, arrive_sem.at[c])
        slots = arrived[c].reshape(total_slots, values)
        placed = jnp.dot(place[...], slots, preferred_element_type=F32).astype(BF16)
        for block in range(BLOCKS):
            for pair in range(NODE // 2):
                stacked[pl.ds(pair * elements, elements), pl.ds(block * 128, 128)] = placed[
                    block * elements : (block + 1) * elements, pair * 128 : (pair + 1) * 128
                ]
        if c == 0:
            loads[COMPONENTS].wait()
            loads[COMPONENTS + 1].wait()

        def group_step(step, carry):
            group = (me_y // GROUP + step) % groups
            here = pl.ds(pl.multiple_of(group * rows, rows), rows)
            even = jnp.dot(fourier_here[0, here], stacked[...], preferred_element_type=F32)
            odd = jnp.dot(fourier_here[1, here], stacked[...], preferred_element_type=F32)
            lane = lax.broadcasted_iota(jnp.int32, even.shape, 1)
            mixed = jnp.where(lane % 128 < 64, even, odd).astype(BF16)
            result = jnp.dot(mixed, plane_here[...], preferred_element_type=F32).astype(BF16)
            coeffs[c, pl.ds(group * GROUP, GROUP)] = result.reshape(GROUP, PADDED, 256)

            def spread(member, inner):
                peer = group * GROUP + (me_y + member) % GROUP

                @pl.when(peer != me_y)
                def _():
                    pltpu.make_async_remote_copy(
                        src_ref=coeffs.at[c, peer],
                        dst_ref=received.at[c, me_y],
                        send_sem=spread_sem.at[c],
                        recv_sem=receive_sem.at[c],
                        device_id={"py": peer},
                        device_id_type=MESH,
                    ).start()

                return inner

            lax.fori_loop(0, GROUP, spread, 0)
            return carry

        lax.fori_loop(0, groups, group_step, 0)
        received[c, me_y] = coeffs[c, me_y]

    pack(0)
    pl.semaphore_wait(barrier, n_pz - 1 + n_py - 1)
    send(0)
    local = lax.broadcasted_iota(jnp.int32, (place.shape[0], total_slots), 0)
    place[...] = jnp.where(local == arrival_slots[...], 1.0, 0.0).astype(BF16)
    for c in range(COMPONENTS):
        if c + 1 < COMPONENTS:
            pack(c + 1)
            send(c + 1)
        transform(c)
    for c in range(COMPONENTS):
        wait_for(outgoing.at[c], n_pz - 1, send_sem.at[c])
        wait_for(coeffs.at[c], n_py - 1, spread_sem.at[c])
        wait_for(received.at[c], n_py - 1, receive_sem.at[c])


def transfer(n_py, n_pz, nodal, counts, send_slots, arrival_slots):
    capacity, values = nodal.shape[1:]
    total_slots = n_pz * SLOTS
    elements = total_slots // 2 // BLOCKS
    fourier = jnp.asarray(fourier_table(n_py, elements))
    plane = jnp.asarray(plane_table())
    vmem = pl.BlockSpec(memory_space=pltpu.VMEM)
    anywhere = pl.BlockSpec(memory_space=pl.ANY)
    return pl.pallas_call(
        functools.partial(transfer_kernel, n_py, n_pz),
        out_shape=jax.ShapeDtypeStruct((COMPONENTS, n_py, PADDED, 256), BF16),
        in_specs=[anywhere, vmem, vmem, vmem, anywhere, anywhere],
        out_specs=vmem,
        scratch_shapes=[
            pltpu.VMEM((COMPONENTS, capacity, values), BF16),
            pltpu.VMEM(fourier.shape, BF16),
            pltpu.VMEM(plane.shape, BF16),
            pltpu.VMEM((total_slots, capacity), BF16),
            pltpu.VMEM((total_slots // 2, total_slots), BF16),
            pltpu.VMEM((values, values), BF16),
            pltpu.VMEM((COMPONENTS, n_pz, SLOTS, values), BF16),
            pltpu.VMEM((COMPONENTS, n_pz, SLOTS, values), BF16),
            pltpu.VMEM((NODE // 2 * elements, BLOCKS * 128), BF16),
            pltpu.VMEM((COMPONENTS, n_py, PADDED, 256), BF16),
            pltpu.SemaphoreType.DMA((COMPONENTS + 2,)),
            pltpu.SemaphoreType.DMA((COMPONENTS,)),
            pltpu.SemaphoreType.DMA((COMPONENTS,)),
            pltpu.SemaphoreType.DMA((COMPONENTS,)),
            pltpu.SemaphoreType.DMA((COMPONENTS,)),
        ],
        compiler_params=pltpu.CompilerParams(
            collective_id=0, has_side_effects=True, vmem_limit_bytes=40 * 1024 * 1024
        ),
    )(nodal, counts, send_slots, arrival_slots, fourier, plane)


def assemble_kernel(received, out, here, spread, load_sem, store_sem):
    bands = received.shape[1]
    granule = lax.broadcasted_iota(jnp.int32, (PADDED, 128), 1) // 16
    loads = [
        pltpu.make_async_copy(received.at[c], here.at[c], load_sem.at[c]) for c in range(COMPONENTS)
    ]
    for load in loads:
        load.start()
    stores = []
    for c in range(COMPONENTS):
        loads[c].wait()
        for half in range(bands // 8):
            for layer in range(2):
                tiles = [
                    here[c, half * 8 + band, :, pl.ds(layer * 128, 128)].astype(F32)
                    for band in range(8)
                ]
                for step in (1, 2, 4):
                    low = granule % (2 * step) < step
                    turned = list(tiles)
                    for at in range(8):
                        if at & step == 0:
                            first, second = tiles[at], tiles[at + step]
                            turned[at] = jnp.where(low, first, pltpu.roll(second, 16 * step, 1))
                            turned[at + step] = jnp.where(
                                low, pltpu.roll(first, 128 - 16 * step, 1), second
                            )
                    tiles = turned
                for at in range(8):
                    rows = pl.ds(layer * 8 + at, USED, stride=16)
                    spread[c, half, rows, :] = tiles[at][:USED]
            store = pltpu.make_async_copy(
                spread.at[c, half], out.at[c, :, pl.ds(half * 128, 128)], store_sem.at[c, half]
            )
            store.start()
            stores.append(store)
    for store in stores:
        store.wait()


def assemble(received):
    n_py = received.shape[1]
    halves = n_py // 8
    return pl.pallas_call(
        assemble_kernel,
        out_shape=jax.ShapeDtypeStruct((COMPONENTS, USED * 16, n_py * 16), F32),
        in_specs=[pl.BlockSpec(memory_space=pl.ANY)],
        out_specs=pl.BlockSpec(memory_space=pl.ANY),
        scratch_shapes=[
            pltpu.VMEM(received.shape, BF16),
            pltpu.VMEM((COMPONENTS, halves, USED * 16, 128), F32),
            pltpu.SemaphoreType.DMA((COMPONENTS,)),
            pltpu.SemaphoreType.DMA((COMPONENTS, halves)),
        ],
        compiler_params=pltpu.CompilerParams(vmem_limit_bytes=24 * 1024 * 1024),
    )(received)


def solution(mesh):
    n_py, n_pz = mesh.shape["py"], mesh.shape["pz"]

    def on_device(nodal, element_counts, send_slots, arrival_slots):
        turned = nodal[0].transpose(1, 0, 2)
        received = transfer(n_py, n_pz, turned, element_counts, send_slots, arrival_slots)
        spectra = assemble(received)
        return spectra.reshape(COMPONENTS, 2, MODES, 16, -1)

    placed = (P("py", "pz", None, None), P("py", "pz"), P("py", "pz"), P("py", "pz"))
    return jax.shard_map(
        on_device,
        mesh=mesh,
        in_specs=placed,
        out_specs=P(None, None, "py", "pz", None),
        check_vma=False,
    )
```

time: 186 us -> 68.3 us (0.37)
  local copies, waits for them, and re-layouts: 86 us -> 4.68 us
  Pallas kernels: 0 us -> 62.7 us
  blocking collectives: 36.3 us -> 0 us
  waiting for transfers between devices: 33 us -> 0 us
  starting transfers between devices: 13.8 us -> 0 us
  other arithmetic: 10.3 us -> 0 us
  matrix products: 4.72 us -> 0 us
    pallas_call x0 -> x2, Pallas kernels: none -> 62.7 us  [the longest x1 60.7 us: transfer(): pl.pallas_call(functools.partial(transfer_kernel, n_py, n_pz), out_shape=...]
    all_to_all x1 -> x0, blocking collectives: 36.3 us -> none  [on_device(): lax.all_to_all(spectra, 'py', split_axis=2, concat_axis=4, tiled=True)]
    all_to_all x1 -> x0, waiting for transfers between devices: 33 us -> none  [on_device(): lax.all_to_all(outgoing, 'pz', split_axis=0, concat_axis=0, tiled=True)]
    reshape x3 -> x0, local copies, waits for them, and re-layouts: 25.8 us -> none  [the longest x1 18.8 us: on_device(): shaped.transpose(3, 2, 6, 0, 4, 1, 5)]
    all_to_all x4 -> x0, local copies, waits for them, and re-layouts: 20.8 us -> none  [the longest x3 18 us: on_device(): lax.all_to_all(spectra, 'py', split_axis=2, concat_axis=4, tiled=True)]
    all_to_all x1 -> x0, starting transfers between devices: 13.8 us -> none  [on_device(): lax.all_to_all(outgoing, 'pz', split_axis=0, concat_axis=0, tiled=True)]
    transpose x1 -> x0, local copies, waits for them, and re-layouts: 9.25 us -> none  [on_device(): shaped.transpose(3, 2, 6, 0, 4, 1, 5)]
    gather x4 -> x0, local copies, waits for them, and re-layouts: 8.35 us -> none  [the longest x3 4.51 us: on_device(): placed = jnp.take(arrived_rows, slot_of, axis=0)]
  transfers between devices with their start and end apart: 1 -> 0, of which waited for: 1 -> 0; matrix products, arithmetic and copies ran while one was open for 3% -> 0% of each run, Pallas kernels for 0% -> 0%
where the time goes in v1:
time: 68.3 us; the launch traced here: 68 us
  Pallas kernels  62.7 us (92%)
  local copies, waits for them, and re-layouts  4.68 us (7%)
    pallas_call x1, Pallas kernels, transfer(): pl.pallas_call(functools.partial(transfer_kernel, n_py, n_pz), out_shape=...  60.7 us
    unnamed x10, local copies, waits for them, and re-layouts  4.68 us
    pallas_call x1, Pallas kernels, assemble(): pl.pallas_call(assemble_kernel, out_shape=jax.ShapeDtypeStruct((COMPONENT...  1.94 us

profile of v1, /device:TPU:1, one launch (start us, length us, event | category | flops | bytes accessed | tf_op | source)
XLA Modules:
  0.0 68.0 jit_solution(14749802333568336413)
XLA Ops:
  0.7 0.0 copy-start
  0.7 1.3 %copy-done = bf16[1,448,3,512]{3,1,2,0:T(8,128)(2,1)S(1)} copy-done((bf16[1,448,3,512]{3,1,2,0:T(8,128)(2,1)S(1)}, bf16[1,448,3,512]{3,1,2,0:T(8,128)(2,1)}, u32[]{:S(2)}) %copy-start) | copy-done | bytes 1376280
  2.0 0.0 copy-start.1
  2.0 1.0 %copy-done.1 = bf16[2,512,256]{2,1,0:T(8,128)(2,1)S(1)} copy-done((bf16[2,512,256]{2,1,0:T(8,128)(2,1)S(1)}, bf16[2,512,256]{2,1,0:T(8,128)(2,1)}, u32[]{:S(2)}) %copy-start.1) | copy-done | bytes 524312
  3.0 0.0 copy-start.2
  3.0 0.9 %copy-done.2 = bf16[512,256]{1,0:T(8,128)(2,1)S(1)} copy-done((bf16[512,256]{1,0:T(8,128)(2,1)S(1)}, bf16[512,256]{1,0:T(8,128)(2,1)}, u32[]{:S(2)}) %copy-start.2) | copy-done | bytes 262168
  4.0 0.0 copy-start.3
  4.0 0.7 copy-done.3
  4.7 0.0 copy-start.4
  4.7 0.7 copy-done.4
  5.3 60.7 %shard_map.64.received = bf16[3,16,32,256]{3,2,1,0:T(8,128)(2,1)S(1)} custom-call(bf16[3,448,512]{2,1,0:T(8,128)(2,1)S(1)} %bitcast.4, s32[1,1]{1,0:T(1,128)S(6)} %copy.7.counts, s32[1,448]{1,0:T(1,128)S(1)} %copy-done.3, s32[1,512]{1,0:T(1,128)S(1)} %copy-done.4, bf16[2,512,256]{2,1,0:T(8,128)(2,1)S(1)} %copy-done.1, bf16[512,256]{1,0:T(8,128)(2,1)S(1)} %copy-done.2), custom_call_target="tpu_custom_call" | custom-call | tf_op jit(solution)/shard_map/pallas_call | solution.py:233
  66.1 1.9 %shard_map.65 = f32[3,320,256]{2,1,0:T(8,128)} custom-call(bf16[3,16,32,256]{3,2,1,0:T(8,128)(2,1)S(1)} %shard_map.64.received), custom_call_target="tpu_custom_call" | custom-call | tf_op jit(solution)/shard_map/pallas_call | solution.py:304
Async XLA Ops:
  0.7 1.3 %copy-start = (bf16[1,448,3,512]{3,1,2,0:T(8,128)(2,1)S(1)}, bf16[1,448,3,512]{3,1,2,0:T(8,128)(2,1)}, u32[]{:S(2)}) copy-start(bf16[1,448,3,512]{3,1,2,0:T(8,128)(2,1)} %param.6) | copy-start | bytes 4128772
  2.0 1.0 %copy-start.1 = (bf16[2,512,256]{2,1,0:T(8,128)(2,1)S(1)}, bf16[2,512,256]{2,1,0:T(8,128)(2,1)}, u32[]{:S(2)}) copy-start(bf16[2,512,256]{2,1,0:T(8,128)(2,1)} %constant.4.clone.fourier) | copy-start | bytes 1572868
  3.0 0.9 %copy-start.2 = (bf16[512,256]{1,0:T(8,128)(2,1)S(1)}, bf16[512,256]{1,0:T(8,128)(2,1)}, u32[]{:S(2)}) copy-start(bf16[512,256]{1,0:T(8,128)(2,1)} %constant.5.clone.plane) | copy-start | bytes 786436
  4.0 0.7 %copy-start.3 = (s32[1,448]{1,0:T(1,128)S(1)}, s32[1,448]{1,0:T(1,128)}, u32[]{:S(2)}) copy-start(s32[1,448]{1,0:T(1,128)} %send_slots.1) | copy-start | bytes 5380
  4.7 0.7 %copy-start.4 = (s32[1,512]{1,0:T(1,128)S(1)}, s32[1,512]{1,0:T(1,128)}, u32[]{:S(2)}) copy-start(s32[1,512]{1,0:T(1,128)} %arrival_slots.1) | copy-start | bytes 6148

commit v2 on v1

v2 whole, which is shorter than its diff:
```python
import functools
import math

import jax
import jax.numpy as jnp
import ml_dtypes
import numpy as np
from jax import lax
from jax.experimental import pallas as pl
from jax.experimental.pallas import tpu as pltpu
from jax.sharding import PartitionSpec as P

NODE = 8
YE = 2
LZ = 2
BLOCKS = YE * LZ
COMPONENTS = 3
SLOTS = 16
X_RING = 4
MODES = 10
USED = 2 * MODES
PADDED = 32
GROUP = 4
ROWS = 24
WAVES = 2 * COMPONENTS
WIDTH = NODE**3 // 2
BF16 = jnp.bfloat16
F32 = jnp.float32
MESH = pl.DeviceIdType.MESH


def lobatto_points(number):
    degree = number - 1
    points = np.cos(np.pi * np.arange(number) / degree)
    for sweeps in range(60):
        older_poly = np.ones(number)
        newer_poly = points.copy()
        for degree_now in range(2, degree + 1):
            older_poly, newer_poly = (
                newer_poly,
                ((2 * degree_now - 1) * points * newer_poly - (degree_now - 1) * older_poly)
                / degree_now,
            )
        points = points - (points * newer_poly - older_poly) / (number * newer_poly)
    return np.sort(points)


def vandermonde(number):
    gauss_points = lobatto_points(number)
    uniform = -1.0 + (2.0 * np.arange(number) + 1.0) / number
    columns_list = []
    for column in range(number):
        same = np.arange(number) == column
        numer = np.where(same[None, :], 1.0, uniform[:, None] - gauss_points[None, :])
        denom = np.where(same, 1.0, gauss_points[column] - gauss_points)
        columns_list.append(np.prod(numer / denom[None, :], axis=1))
    return np.stack(columns_list, axis=1)


def fourier_table(bands, elements):
    length = elements * NODE
    wavenumber = np.arange(bands * MODES)[:, None]
    angles = (wavenumber * np.arange(length)[None, :] % length) * (2.0 * np.pi / length)
    dft = np.stack([np.cos(angles), -np.sin(angles)]) / math.sqrt(length)
    dft = dft.reshape(2, bands, MODES, elements, NODE)
    nodes = np.einsum("tikeh,hn->itkne", dft, vandermonde(NODE))
    table = np.zeros((bands, PADDED, NODE, elements))
    table[:, :USED] = nodes.reshape(bands, USED, NODE, elements)
    return table.reshape(bands * PADDED, NODE * elements).astype(ml_dtypes.bfloat16)


def plane_table():
    lagrange = vandermonde(NODE)
    table = np.einsum("fu,gv,hw->uvhwfg", lagrange, lagrange, np.eye(NODE))
    table = table.reshape(NODE**3, NODE, 2, NODE // 2, NODE).transpose(2, 0, 1, 3, 4)
    return table.reshape(2, NODE**3, NODE**3 // 2).astype(ml_dtypes.bfloat16)


def exchange(tiles, index_bit, lane_bit, width):
    lane = lax.broadcasted_iota(jnp.int32, tiles[0].shape, 1)
    shift = lane_bit * width
    low = lane % (2 * shift) < shift
    turned = list(tiles)
    for at in range(len(tiles)):
        if at & index_bit == 0:
            first, second = tiles[at], tiles[at + index_bit]
            turned[at] = jnp.where(low, first, pltpu.roll(second, shift, 1))
            turned[at + index_bit] = jnp.where(low, pltpu.roll(first, 128 - shift, 1), second)
    return turned


def transfer_kernel(
    n_py, n_pz, nodal, counts, send_slots, arrival_slots, fourier, plane, out,
    nodes, counts_here, send_here, arrival_here, fourier_here, plane_here, pick, place,
    outgoing, relayed, arrived, stacked, coeffs, received, ordered, final,
    load_sem, send_sem, relay_sem, forward_sem, arrive_sem, spread_sem, receive_sem, store_sem,
):
    me_y = lax.axis_index("py")
    me_z = lax.axis_index("pz")
    z_ring = n_pz // X_RING
    my_plane, my_column = me_z // X_RING, me_z % X_RING
    capacity = nodes.shape[1]
    elements = place.shape[0] // BLOCKS
    total_slots = n_pz * SLOTS

    barrier = pltpu.get_barrier_semaphore()

    def greet_z(step, carry):
        pl.semaphore_signal(
            barrier, inc=1, device_id={"pz": (me_z + step) % n_pz}, device_id_type=MESH
        )
        return carry

    def greet_y(step, carry):
        pl.semaphore_signal(
            barrier, inc=1, device_id={"py": (me_y + step) % n_py}, device_id_type=MESH
        )
        return carry

    pairs = [
        (send_slots, send_here),
        (counts, counts_here),
        (nodal.at[0], nodes.at[0]),
        (plane, plane_here),
        (arrival_slots, arrival_here),
        (nodal.at[1], nodes.at[1]),
        (nodal.at[2], nodes.at[2]),
        (fourier, fourier_here),
    ]
    loads = [
        pltpu.make_async_copy(source, here, load_sem.at[at])
        for at, (source, here) in enumerate(pairs)
    ]
    for load in loads:
        load.start()
    lax.fori_loop(1, n_pz, greet_z, 0)
    lax.fori_loop(1, n_py, greet_y, 0)

    loads[0].wait()
    loads[1].wait()
    column = lax.broadcasted_iota(jnp.int32, (1, capacity), 1)
    target = jnp.where(column < counts_here[...], send_here[...], -1)
    row = lax.broadcasted_iota(jnp.int32, (total_slots, capacity), 0)
    pick[...] = jnp.where(row == target, 1.0, 0.0).astype(BF16)

    def pack(wave):
        c, half = wave // 2, wave % 2
        turned = jnp.dot(nodes[c], plane_here[half], preferred_element_type=F32).astype(BF16)
        packed = jnp.dot(pick[...], turned, preferred_element_type=F32).astype(BF16)
        outgoing[wave] = packed.reshape(n_pz, SLOTS, WIDTH)

    def peer_at(plane_step, column_step):
        peer_plane = (my_plane + plane_step + z_ring) % z_ring
        return peer_plane * X_RING + (my_column + column_step + X_RING) % X_RING

    def send_to(wave, plane_step, column_step):
        peer = peer_at(plane_step, column_step)
        pltpu.make_async_remote_copy(
            src_ref=outgoing.at[wave, peer],
            dst_ref=arrived.at[wave, me_z],
            send_sem=send_sem.at[wave],
            recv_sem=arrive_sem.at[wave],
            device_id={"pz": peer},
            device_id_type=MESH,
        ).start()

    quarter = z_ring // 4

    def send_opposite(wave):
        def opposite(step, carry):
            way = (1 - step // 2 * 2) * quarter
            pltpu.make_async_remote_copy(
                src_ref=outgoing.at[wave, peer_at(2 * quarter, step)],
                dst_ref=relayed.at[wave, step],
                send_sem=send_sem.at[wave],
                recv_sem=relay_sem.at[wave],
                device_id={"pz": peer_at(way, step)},
                device_id_type=MESH,
            ).start()
            return carry

        lax.fori_loop(0, X_RING, opposite, 0)

    def send(wave):
        def far(step, carry):
            turn = step // X_RING
            send_to(wave, (turn + 2) // 2 * (1 - 2 * (turn % 2)), step % X_RING)
            return carry

        def near(step, carry):
            send_to(wave, 0, step)
            return carry

        lax.fori_loop(0, (z_ring - 2) * X_RING, far, 0)
        lax.fori_loop(1, X_RING, near, 0)
        arrived[wave, me_z] = outgoing[wave, me_z]

    def forward(wave):
        wait_for(relayed.at[wave], X_RING, relay_sem.at[wave])

        def onward(step, carry):
            way = (1 - step // 2 * 2) * quarter
            pltpu.make_async_remote_copy(
                src_ref=relayed.at[wave, step],
                dst_ref=arrived.at[wave, peer_at(-way, -step)],
                send_sem=forward_sem.at[wave],
                recv_sem=arrive_sem.at[wave],
                device_id={"pz": peer_at(way, 0)},
                device_id_type=MESH,
            ).start()
            return carry

        lax.fori_loop(0, X_RING, onward, 0)

    def wait_for(ref, blocks, sem):
        part = ref.at[pl.ds(0, blocks)]
        pltpu.make_async_copy(part, part, sem).wait()

    rows = GROUP * PADDED
    groups = n_py // GROUP

    def transform(wave):
        slots = arrived[wave].reshape(total_slots, WIDTH)
        placed = jnp.dot(place[...], slots, preferred_element_type=F32)
        for quad in range(2):
            tiles = [
                placed[block * elements : (block + 1) * elements, quad * 128 : (quad + 1) * 128]
                for block in range(BLOCKS)
            ]
            tiles = exchange(exchange(tiles, 1, 1, 32), 2, 2, 32)
            for at, tile in enumerate(tiles):
                stacked[pl.ds((quad * 4 + at) * elements, elements), :] = tile.astype(BF16)

        def group_step(step, carry):
            group = (me_y // GROUP + step) % groups
            here = pl.ds(pl.multiple_of(group * rows, rows), rows)
            result = jnp.dot(fourier_here[here], stacked[...], preferred_element_type=F32)
            coeffs[wave, pl.ds(group * GROUP, GROUP)] = result.astype(BF16).reshape(
                GROUP, PADDED, 128
            )

            def spread(member, inner):
                peer = group * GROUP + (me_y + member) % GROUP

                @pl.when(peer != me_y)
                def _():
                    pltpu.make_async_remote_copy(
                        src_ref=coeffs.at[wave, peer],
                        dst_ref=received.at[wave, me_y],
                        send_sem=spread_sem.at[wave],
                        recv_sem=receive_sem.at[wave],
                        device_id={"py": peer},
                        device_id_type=MESH,
                    ).start()

                return inner

            lax.fori_loop(0, GROUP, spread, 0)
            return carry

        lax.fori_loop(0, groups, group_step, 0)
        received[wave, me_y] = coeffs[wave, me_y]

    def put_in_order(wave):
        wait_for(received.at[wave], n_py - 1, receive_sem.at[wave])
        c, half = wave // 2, wave % 2

        def side_step(side, carry):
            tiles = [received[wave, side * 8 + band].astype(F32)[:ROWS] for band in range(8)]
            for index_bit, lane_bit in ((4, 8), (2, 4), (1, 2), (2, 1)):
                tiles = exchange(tiles, index_bit, lane_bit, 8)
            for at in range(8):
                z = at // 4 * 8 + half * 4 + at % 2 * 2 + at // 2 % 2
                ordered[c, side, pl.ds(z, USED, stride=16), :] = tiles[at][:USED]
            return carry

        lax.fori_loop(0, n_py // 8, side_step, 0)

    def store(c):
        for side in range(n_py // 8):
            final[c, :, pl.ds(side * 128, 128)] = ordered[c, side].astype(BF16)
        copy = pltpu.make_async_copy(final.at[c], out.at[c], store_sem.at[c])
        copy.start()
        return copy

    loads[2].wait()
    loads[3].wait()
    pack(0)
    pl.semaphore_wait(barrier, n_pz - 1 + n_py - 1)
    send_opposite(0)
    pack(1)
    send_opposite(1)
    send(0)
    loads[5].wait()
    pack(2)
    send_opposite(2)
    pack(3)
    send_opposite(3)
    forward(0)
    forward(1)
    send(1)
    loads[6].wait()
    pack(4)
    pack(5)
    loads[4].wait()
    local = lax.broadcasted_iota(jnp.int32, (place.shape[0], total_slots), 0)
    place[...] = jnp.where(local == arrival_here[...], 1.0, 0.0).astype(BF16)
    loads[7].wait()
    for wave in range(WAVES):
        wait_for(arrived.at[wave], n_pz - 1, arrive_sem.at[wave])
        if wave + 4 < WAVES:
            send_opposite(wave + 4)
        if wave + 3 < WAVES:
            forward(wave + 2)
            send(wave + 2)
        transform(wave)
        if wave + 3 == WAVES:
            forward(wave + 2)
            send(wave + 2)
        if wave >= 3:
            put_in_order(wave - 3)
    copies = [store(0)]
    put_in_order(3)
    copies.append(store(1))
    put_in_order(4)
    put_in_order(5)
    copies.append(store(2))
    for wave in range(WAVES):
        wait_for(outgoing.at[wave], n_pz - 1, send_sem.at[wave])
        wait_for(relayed.at[wave], X_RING, forward_sem.at[wave])
        wait_for(coeffs.at[wave], n_py - 1, spread_sem.at[wave])
    for copy in copies:
        copy.wait()


def transfer(n_py, n_pz, nodal, counts, send_slots, arrival_slots):
    capacity, values = nodal.shape[1:]
    total_slots = n_pz * SLOTS
    elements = total_slots // 2 // BLOCKS
    fourier = jnp.asarray(fourier_table(n_py, elements))
    plane = jnp.asarray(plane_table())
    anywhere = pl.BlockSpec(memory_space=pl.ANY)
    return pl.pallas_call(
        functools.partial(transfer_kernel, n_py, n_pz),
        out_shape=jax.ShapeDtypeStruct((COMPONENTS, USED * 16, n_py * 16), BF16),
        in_specs=[anywhere] * 6,
        out_specs=anywhere,
        scratch_shapes=[
            pltpu.VMEM((COMPONENTS, capacity, values), BF16),
            pltpu.VMEM(counts.shape, jnp.int32),
            pltpu.VMEM(send_slots.shape, jnp.int32),
            pltpu.VMEM(arrival_slots.shape, jnp.int32),
            pltpu.VMEM(fourier.shape, BF16),
            pltpu.VMEM(plane.shape, BF16),
            pltpu.VMEM((total_slots, capacity), BF16),
            pltpu.VMEM((total_slots // 2, total_slots), BF16),
            pltpu.VMEM((WAVES, n_pz, SLOTS, WIDTH), BF16),
            pltpu.VMEM((WAVES, X_RING, SLOTS, WIDTH), BF16),
            pltpu.VMEM((WAVES, n_pz, SLOTS, WIDTH), BF16),
            pltpu.VMEM((NODE * elements, 128), BF16),
            pltpu.VMEM((WAVES, n_py, PADDED, 128), BF16),
            pltpu.VMEM((WAVES, n_py, PADDED, 128), BF16),
            pltpu.VMEM((COMPONENTS, n_py // 8, USED * 16, 128), F32),
            pltpu.VMEM((COMPONENTS, USED * 16, n_py * 16), BF16),
            pltpu.SemaphoreType.DMA((8,)),
            pltpu.SemaphoreType.DMA((WAVES,)),
            pltpu.SemaphoreType.DMA((WAVES,)),
            pltpu.SemaphoreType.DMA((WAVES,)),
            pltpu.SemaphoreType.DMA((WAVES,)),
            pltpu.SemaphoreType.DMA((WAVES,)),
            pltpu.SemaphoreType.DMA((WAVES,)),
            pltpu.SemaphoreType.DMA((COMPONENTS,)),
        ],
        compiler_params=pltpu.CompilerParams(
            collective_id=0, has_side_effects=True, vmem_limit_bytes=60 * 1024 * 1024
        ),
    )(nodal, counts, send_slots, arrival_slots, fourier, plane)


def solution(mesh):
    n_py, n_pz = mesh.shape["py"], mesh.shape["pz"]

    def on_device(nodal, element_counts, send_slots, arrival_slots):
        turned = nodal[0].transpose(1, 0, 2)
        spectra = transfer(n_py, n_pz, turned, element_counts, send_slots, arrival_slots)
        return spectra.astype(F32).reshape(COMPONENTS, 2, MODES, 16, -1)

    placed = (P("py", "pz", None, None), P("py", "pz"), P("py", "pz"), P("py", "pz"))
    return jax.shard_map(
        on_device,
        mesh=mesh,
        in_specs=placed,
        out_specs=P(None, None, "py", "pz", None),
        check_vma=False,
    )
```

time: 68.3 us -> 65.9 us (0.965)
  local copies, waits for them, and re-layouts: 4.68 us -> 0 us
  other arithmetic: 0 us -> 2.1 us
    unnamed x10 -> x0, local copies, waits for them, and re-layouts: 4.68 us -> none
    pallas_call x1, Pallas kernels: 60.7 us -> 62.9 us  [transfer(): pl.pallas_call(functools.partial(transfer_kernel, n_py, n_pz), out_shape=...]
    reshape x0 -> x1, other arithmetic: none -> 2.1 us  [on_device(): return spectra.astype(F32).reshape(COMPONENTS, 2, MODES, 16, -1)]
    pallas_call x1 -> x0, Pallas kernels: 1.94 us -> none  [assemble(): pl.pallas_call(assemble_kernel, out_shape=jax.ShapeDtypeStruct((COMPONENT...]
where the time goes in v2:
time: 65.9 us; the launch traced here: 65.7 us
  Pallas kernels  62.9 us (95%)
  other arithmetic  2.1 us (3%)
  between operations  0.66 us (1%)
    pallas_call x1, Pallas kernels, transfer(): pl.pallas_call(functools.partial(transfer_kernel, n_py, n_pz), out_shape=...  62.9 us
    reshape x1, other arithmetic, on_device(): return spectra.astype(F32).reshape(COMPONENTS, 2, MODES, 16, -1)  2.1 us

profile of v2, /device:TPU:1, one launch (start us, length us, event | category | flops | bytes accessed | tf_op | source)
XLA Modules:
  0.0 65.7 jit_solution(12098290444961377627)
XLA Ops:
  0.7 62.9 %shard_map.64 = bf16[3,320,256]{2,1,0:T(8,128)(2,1)} custom-call(bf16[3,448,512]{2,1,0:T(8,128)(2,1)} %bitcast.6, s32[1,1]{1,0:T(1,128)S(6)} %copy.7.counts, s32[1,448]{1,0:T(1,128)} %send_slots.1, s32[1,512]{1,0:T(1,128)} %arrival_slots.1, bf16[512,512]{1,0:T(8,128)(2,1)} %constant.4.clone.fourier, bf16[2,512,256]{2,1,0:T(8,128)(2,1)} %constant.5.clone.plane), custom_call_target="tpu_custom_call" | custom-call | tf_op jit(solution)/shard_map/pallas_call | solution.py:343
  63.6 2.1 %convert.1 = f32[3,2,10,16,256]{4,3,2,1,0:T(8,128)} convert(bf16[3,2,10,16,256]{4,3,2,1,0:T(8,128)(2,1)} %bitcast.5) | non-fusion elementwise | flops 245760 | bytes 1474560 | tf_op jit(solution)/shard_map/reshape | solution.py:386

commit v3 on v2

--- a/solution.py
+++ b/solution.py
@@ -92,7 +92,7 @@
 def transfer_kernel(
     n_py, n_pz, nodal, counts, send_slots, arrival_slots, fourier, plane, out,
     nodes, counts_here, send_here, arrival_here, fourier_here, plane_here, pick, place,
-    outgoing, relayed, arrived, stacked, coeffs, received, ordered, final,
+    outgoing, relayed, arrived, stacked, coeffs, received, ordered,
     load_sem, send_sem, relay_sem, forward_sem, arrive_sem, spread_sem, receive_sem, store_sem,
 ):
     me_y = lax.axis_index("py")
@@ -183,8 +183,9 @@
 
     def send(wave):
         def far(step, carry):
-            turn = step // X_RING
-            send_to(wave, (turn + 2) // 2 * (1 - 2 * (turn % 2)), step % X_RING)
+            turn = step % (z_ring - 2)
+            side = 1 - (turn + me_y) % 2 * 2
+            send_to(wave, side * (turn // 2 + 1), side * (step // (z_ring - 2)))
             return carry
 
         def near(step, carry):
@@ -277,11 +278,15 @@
         lax.fori_loop(0, n_py // 8, side_step, 0)
 
     def store(c):
-        for side in range(n_py // 8):
-            final[c, :, pl.ds(side * 128, 128)] = ordered[c, side].astype(BF16)
-        copy = pltpu.make_async_copy(final.at[c], out.at[c], store_sem.at[c])
-        copy.start()
-        return copy
+        copies = [
+            pltpu.make_async_copy(
+                ordered.at[c, side], out.at[c, :, pl.ds(side * 128, 128)], store_sem.at[c, side]
+            )
+            for side in range(n_py // 8)
+        ]
+        for copy in copies:
+            copy.start()
+        return copies
 
     loads[2].wait()
     loads[3].wait()
@@ -319,12 +324,12 @@
             send(wave + 2)
         if wave >= 3:
             put_in_order(wave - 3)
-    copies = [store(0)]
+    copies = store(0)
     put_in_order(3)
-    copies.append(store(1))
+    copies += store(1)
     put_in_order(4)
     put_in_order(5)
-    copies.append(store(2))
+    copies += store(2)
     for wave in range(WAVES):
         wait_for(outgoing.at[wave], n_pz - 1, send_sem.at[wave])
         wait_for(relayed.at[wave], X_RING, forward_sem.at[wave])
@@ -342,7 +347,7 @@
     anywhere = pl.BlockSpec(memory_space=pl.ANY)
     return pl.pallas_call(
         functools.partial(transfer_kernel, n_py, n_pz),
-        out_shape=jax.ShapeDtypeStruct((COMPONENTS, USED * 16, n_py * 16), BF16),
+        out_shape=jax.ShapeDtypeStruct((COMPONENTS, USED * 16, n_py * 16), F32),
         in_specs=[anywhere] * 6,
         out_specs=anywhere,
         scratch_shapes=[
@@ -361,7 +366,6 @@
             pltpu.VMEM((WAVES, n_py, PADDED, 128), BF16),
             pltpu.VMEM((WAVES, n_py, PADDED, 128), BF16),
             pltpu.VMEM((COMPONENTS, n_py // 8, USED * 16, 128), F32),
-            pltpu.VMEM((COMPONENTS, USED * 16, n_py * 16), BF16),
             pltpu.SemaphoreType.DMA((8,)),
             pltpu.SemaphoreType.DMA((WAVES,)),
             pltpu.SemaphoreType.DMA((WAVES,)),
@@ -369,7 +373,7 @@
             pltpu.SemaphoreType.DMA((WAVES,)),
             pltpu.SemaphoreType.DMA((WAVES,)),
             pltpu.SemaphoreType.DMA((WAVES,)),
-            pltpu.SemaphoreType.DMA((COMPONENTS,)),
+            pltpu.SemaphoreType.DMA((COMPONENTS, n_py // 8)),
         ],
         compiler_params=pltpu.CompilerParams(
             collective_id=0, has_side_effects=True, vmem_limit_bytes=60 * 1024 * 1024
@@ -383,7 +387,7 @@
     def on_device(nodal, element_counts, send_slots, arrival_slots):
         turned = nodal[0].transpose(1, 0, 2)
         spectra = transfer(n_py, n_pz, turned, element_counts, send_slots, arrival_slots)
-        return spectra.astype(F32).reshape(COMPONENTS, 2, MODES, 16, -1)
+        return spectra.reshape(COMPONENTS, 2, MODES, 16, -1)
 
     placed = (P("py", "pz", None, None), P("py", "pz"), P("py", "pz"), P("py", "pz"))
     return jax.shard_map(

time: 65.9 us -> 65.4 us (level)
  local copies, waits for them, and re-layouts: 0 us -> 2.26 us
  other arithmetic: 2.1 us -> 0 us
    unnamed x0 -> x1, local copies, waits for them, and re-layouts: none -> 2.26 us
    reshape x1 -> x0, other arithmetic: 2.1 us -> none  [on_device(): return spectra.astype(F32).reshape(COMPONENTS, 2, MODES, 16, -1)]
where the time goes in v3:
time: 65.4 us; the launch traced here: 65.2 us
  Pallas kernels  62.3 us (95%)
  local copies, waits for them, and re-layouts  2.26 us (3%)
  between operations  0.66 us (1%)
    pallas_call x1, Pallas kernels, transfer(): pl.pallas_call(functools.partial(transfer_kernel, n_py, n_pz), out_shape=...  62.3 us
    unnamed x1, local copies, waits for them, and re-layouts  2.26 us

profile of v3, /device:TPU:1, one launch (start us, length us, event | category | flops | bytes accessed | tf_op | source)
XLA Modules:
  0.0 65.2 jit_solution(8718956656289338426)
XLA Ops:
  0.7 62.3 %shard_map.64 = f32[3,320,256]{2,1,0:T(8,128)} custom-call(bf16[3,448,512]{2,1,0:T(8,128)(2,1)} %bitcast.5, s32[1,1]{1,0:T(1,128)S(6)} %copy.8.counts, s32[1,448]{1,0:T(1,128)} %send_slots.1, s32[1,512]{1,0:T(1,128)} %arrival_slots.1, bf16[512,512]{1,0:T(8,128)(2,1)} %constant.4.clone.fourier, bf16[2,512,256]{2,1,0:T(8,128)(2,1)} %constant.5.clone.plane), custom_call_target="tpu_custom_call" | custom-call | tf_op jit(solution)/shard_map/pallas_call | solution.py:348
  63.0 2.3 %copy.9 = f32[3,2,10,16,256]{4,3,2,1,0:T(8,128)} copy(f32[3,2,10,16,256]{4,3,2,1,0:T(8,128)} %bitcast.4) | data formatting | bytes 1966080

commit v4 on v3

v4 whole, which is shorter than its diff:
```python
import functools
import math

import jax
import jax.numpy as jnp
import ml_dtypes
import numpy as np
from jax import lax
from jax.experimental import pallas as pl
from jax.experimental.pallas import tpu as pltpu
from jax.sharding import PartitionSpec as P

NODE = 8
YE = 2
LZ = 2
BLOCKS = YE * LZ
COMPONENTS = 3
SLOTS = 16
X_RING = 4
MODES = 10
USED = 2 * MODES
TILE = 16
LEFT = USED - TILE
GROUP = 8
WAVES = ((0, 0, 2), (1, 0, 2), (2, 0, 1), (2, 1, 1))
PARTS = ((0, 0, 3), (1, 0, 3), (2, 0, 1), (2, 1, 2))
WIDTH = NODE**3 // 2
BF16 = jnp.bfloat16
F32 = jnp.float32
MESH = pl.DeviceIdType.MESH


def lobatto_points(number):
    degree = number - 1
    points = np.cos(np.pi * np.arange(number) / degree)
    for sweeps in range(60):
        older_poly = np.ones(number)
        newer_poly = points.copy()
        for degree_now in range(2, degree + 1):
            older_poly, newer_poly = (
                newer_poly,
                ((2 * degree_now - 1) * points * newer_poly - (degree_now - 1) * older_poly)
                / degree_now,
            )
        points = points - (points * newer_poly - older_poly) / (number * newer_poly)
    return np.sort(points)


def vandermonde(number):
    gauss_points = lobatto_points(number)
    uniform = -1.0 + (2.0 * np.arange(number) + 1.0) / number
    columns_list = []
    for column in range(number):
        same = np.arange(number) == column
        numer = np.where(same[None, :], 1.0, uniform[:, None] - gauss_points[None, :])
        denom = np.where(same, 1.0, gauss_points[column] - gauss_points)
        columns_list.append(np.prod(numer / denom[None, :], axis=1))
    return np.stack(columns_list, axis=1)


def fourier_table(bands, elements):
    length = elements * NODE
    wavenumber = np.arange(bands * MODES)[:, None]
    angles = (wavenumber * np.arange(length)[None, :] % length) * (2.0 * np.pi / length)
    dft = np.stack([np.cos(angles), -np.sin(angles)]) / math.sqrt(length)
    dft = dft.reshape(2, bands, MODES, elements, NODE)
    nodes = np.einsum("tikeh,hn->itkne", dft, vandermonde(NODE))
    nodes = nodes.reshape(bands, USED, NODE, elements)
    table = np.zeros((2, bands, TILE, NODE, elements))
    table[0] = nodes[:, :TILE]
    table[1, :, :LEFT] = nodes[:, TILE:]
    return table.reshape(2, bands * TILE, NODE * elements).astype(ml_dtypes.bfloat16)


def plane_table():
    lagrange = vandermonde(NODE)
    table = np.einsum("fu,gv,hw->uvhwfg", lagrange, lagrange, np.eye(NODE))
    table = table.reshape(NODE**3, NODE, 2, NODE // 2, NODE).transpose(2, 0, 1, 3, 4)
    return table.reshape(2, NODE**3, NODE**3 // 2).astype(ml_dtypes.bfloat16)


def exchange(tiles, index_bit, lane_bit, width):
    lane = lax.broadcasted_iota(jnp.int32, tiles[0].shape, 1)
    shift = lane_bit * width
    low = lane % (2 * shift) < shift
    turned = list(tiles)
    for at in range(len(tiles)):
        if at & index_bit == 0:
            first, second = tiles[at], tiles[at + index_bit]
            turned[at] = jnp.where(low, first, pltpu.roll(second, shift, 1))
            turned[at + index_bit] = jnp.where(low, pltpu.roll(first, 128 - shift, 1), second)
    return turned


def transfer_kernel(
    n_py, n_pz, nodal, counts, send_slots, arrival_slots, fourier, plane, out,
    nodes, counts_here, send_here, arrival_here, fourier_here, plane_here, pick, place,
    outgoing, relayed, arrived, stacked, leftover, coeffs, received,
    load_sem, send_sem, relay_sem, forward_sem, arrive_sem, spread_sem, receive_sem,
):
    me_y = lax.axis_index("py")
    me_z = lax.axis_index("pz")
    z_ring = n_pz // X_RING
    my_plane, my_column = me_z // X_RING, me_z % X_RING
    capacity = nodes.shape[1]
    elements = place.shape[0] // BLOCKS
    total_slots = n_pz * SLOTS

    barrier = pltpu.get_barrier_semaphore()

    def greet_z(step, carry):
        pl.semaphore_signal(
            barrier, inc=1, device_id={"pz": (me_z + step) % n_pz}, device_id_type=MESH
        )
        return carry

    def greet_y(step, carry):
        pl.semaphore_signal(
            barrier, inc=1, device_id={"py": (me_y + step) % n_py}, device_id_type=MESH
        )
        return carry

    pairs = [
        (send_slots, send_here),
        (counts, counts_here),
        (nodal.at[0], nodes.at[0]),
        (plane, plane_here),
        (arrival_slots, arrival_here),
        (nodal.at[1], nodes.at[1]),
        (nodal.at[2], nodes.at[2]),
        (fourier, fourier_here),
    ]
    loads = [
        pltpu.make_async_copy(source, here, load_sem.at[at])
        for at, (source, here) in enumerate(pairs)
    ]
    for load in loads:
        load.start()
    lax.fori_loop(1, n_pz, greet_z, 0)
    lax.fori_loop(1, n_py, greet_y, 0)

    loads[0].wait()
    loads[1].wait()
    column = lax.broadcasted_iota(jnp.int32, (1, capacity), 1)
    target = jnp.where(column < counts_here[...], send_here[...], -1)
    row = lax.broadcasted_iota(jnp.int32, (total_slots, capacity), 0)
    pick[...] = jnp.where(row == target, 1.0, 0.0).astype(BF16)

    def pack(c):
        for half in range(2):
            turned = jnp.dot(nodes[c], plane_here[half], preferred_element_type=F32).astype(BF16)
            packed = jnp.dot(pick[...], turned, preferred_element_type=F32).astype(BF16)
            outgoing[c, :, half] = packed.reshape(n_pz, SLOTS, WIDTH)

    def peer_at(plane_step, column_step):
        peer_plane = (my_plane + plane_step + z_ring) % z_ring
        return peer_plane * X_RING + (my_column + column_step + X_RING) % X_RING

    def block(ref, wave, device):
        c, first, number = WAVES[wave]
        return ref.at[c, device, pl.ds(first, number)]

    def piece(ref, wave, device):
        c, first, number = PARTS[wave]
        return ref.at[c, device, pl.ds(first, number)]

    def wait_for(part, sem):
        pltpu.make_async_copy(part, part, sem).wait()

    def send_to(wave, plane_step, column_step):
        peer = peer_at(plane_step, column_step)
        pltpu.make_async_remote_copy(
            src_ref=block(outgoing, wave, peer),
            dst_ref=block(arrived, wave, me_z),
            send_sem=send_sem.at[wave],
            recv_sem=arrive_sem.at[wave],
            device_id={"pz": peer},
            device_id_type=MESH,
        ).start()

    quarter = z_ring // 4

    def send_opposite(wave):
        def opposite(step, carry):
            way = (1 - step % 2 * 2) * quarter
            pltpu.make_async_remote_copy(
                src_ref=block(outgoing, wave, peer_at(2 * quarter, step)),
                dst_ref=block(relayed, wave, step),
                send_sem=send_sem.at[wave],
                recv_sem=relay_sem.at[wave],
                device_id={"pz": peer_at(way, step)},
                device_id_type=MESH,
            ).start()
            return carry

        lax.fori_loop(0, X_RING, opposite, 0)

    def send(wave):
        def far(step, carry):
            turn = step % (z_ring - 2)
            side = 1 - (turn + me_y) % 2 * 2
            send_to(wave, side * (turn // 2 + 1), side * (step // (z_ring - 2)))
            return carry

        def near(step, carry):
            send_to(wave, 0, step)
            return carry

        lax.fori_loop(1, X_RING, near, 0)
        lax.fori_loop(0, (z_ring - 2) * X_RING, far, 0)
        c, first, number = WAVES[wave]
        for half in range(first, first + number):
            arrived[c, me_z, half] = outgoing[c, me_z, half]

    def forward(wave):
        wait_for(block(relayed, wave, pl.ds(0, X_RING)), relay_sem.at[wave])

        def onward(step, carry):
            way = (1 - step % 2 * 2) * quarter
            pltpu.make_async_remote_copy(
                src_ref=block(relayed, wave, step),
                dst_ref=block(arrived, wave, peer_at(-way, -step)),
                send_sem=forward_sem.at[wave],
                recv_sem=arrive_sem.at[wave],
                device_id={"pz": peer_at(way, 0)},
                device_id_type=MESH,
            ).start()
            return carry

        lax.fori_loop(0, X_RING, onward, 0)

    def receive(wave):
        wait_for(block(arrived, wave, pl.ds(0, n_pz - 1)), arrive_sem.at[wave])

    rows = GROUP * TILE
    groups = n_py // GROUP

    def transform(c, half):
        slots = arrived[c, :, half].reshape(total_slots, WIDTH)
        placed = jnp.dot(place[...], slots, preferred_element_type=F32)
        for quad in range(2):
            tiles = [
                placed[at * elements : (at + 1) * elements, quad * 128 : (quad + 1) * 128]
                for at in range(BLOCKS)
            ]
            tiles = exchange(exchange(tiles, 1, 1, 32), 2, 2, 32)
            for at, tile in enumerate(tiles):
                stacked[pl.ds((quad * 4 + at) * elements, elements), :] = tile.astype(BF16)

        def group_step(step, carry):
            here = pl.ds(pl.multiple_of(step * rows, rows), rows)
            members = pl.ds(step * GROUP, GROUP)
            result = jnp.dot(fourier_here[0, here], stacked[...], preferred_element_type=F32)
            coeffs[c, members, half] = result.astype(BF16).reshape(GROUP, TILE, 128)
            rest = jnp.dot(fourier_here[1, here], stacked[...], preferred_element_type=F32)
            if half == 0:
                leftover[here] = rest
            else:
                both = leftover[here] + pltpu.roll(rest, LEFT, 0)
                coeffs[c, members, 2] = both.astype(BF16).reshape(GROUP, TILE, 128)
            return carry

        lax.fori_loop(0, groups, group_step, 0)

    def spread(wave):
        c, first, number = PARTS[wave]
        for part in range(first, first + number):
            received[c, me_y, part] = coeffs[c, me_y, part]

        def spread_to(step, carry):
            peer = (me_y + (step + 1) // 2 * (1 - step % 2 * 2) + n_py) % n_py
            pltpu.make_async_remote_copy(
                src_ref=piece(coeffs, wave, peer),
                dst_ref=piece(received, wave, me_y),
                send_sem=spread_sem.at[wave],
                recv_sem=receive_sem.at[wave],
                device_id={"py": peer},
                device_id_type=MESH,
            ).start()
            return carry

        lax.fori_loop(1, n_py, spread_to, 0)

    def gather(wave):
        wait_for(piece(received, wave, pl.ds(0, n_py - 1)), receive_sem.at[wave])

    def put_in_order(c, part):
        def side_step(side, carry):
            tiles = [received[c, side * 8 + band, part].astype(F32) for band in range(8)]
            if part == 2:
                tiles = [tile[: 2 * LEFT] for tile in tiles]
            for index_bit, lane_bit in ((4, 8), (2, 4), (1, 2), (2, 1)):
                tiles = exchange(tiles, index_bit, lane_bit, 8)
            for at in range(8):
                z = at // 4 * 8 + at % 2 * 2 + at // 2 % 2
                if part == 2:
                    for half in range(2):
                        here = pl.ds(TILE * 16 + half * 4 + z, LEFT, stride=16)
                        out[c, side, here, :] = tiles[at][half * LEFT : (half + 1) * LEFT]
                else:
                    out[c, side, pl.ds(part * 4 + z, TILE, stride=16), :] = tiles[at]
            return carry

        lax.fori_loop(0, n_py // 8, side_step, 0)

    loads[2].wait()
    loads[3].wait()
    pack(0)
    pl.semaphore_wait(barrier, n_pz - 1 + n_py - 1)
    send_opposite(0)
    loads[5].wait()
    pack(1)
    send_opposite(1)
    send(0)
    loads[6].wait()
    pack(2)
    send_opposite(2)
    send_opposite(3)
    forward(0)
    forward(1)
    send(1)
    loads[4].wait()
    local = lax.broadcasted_iota(jnp.int32, (place.shape[0], total_slots), 0)
    place[...] = jnp.where(local == arrival_here[...], 1.0, 0.0).astype(BF16)
    loads[7].wait()
    receive(0)
    forward(2)
    send(2)
    transform(0, 0)
    transform(0, 1)
    spread(0)
    receive(1)
    transform(1, 0)
    transform(1, 1)
    spread(1)
    forward(3)
    send(3)
    receive(2)
    transform(2, 0)
    spread(2)
    gather(0)
    for part in range(3):
        put_in_order(0, part)
    receive(3)
    transform(2, 1)
    spread(3)
    gather(1)
    for part in range(3):
        put_in_order(1, part)
    gather(2)
    put_in_order(2, 0)
    gather(3)
    put_in_order(2, 1)
    put_in_order(2, 2)
    for wave in range(len(WAVES)):
        wait_for(block(outgoing, wave, pl.ds(0, n_pz - 1)), send_sem.at[wave])
        wait_for(block(relayed, wave, pl.ds(0, X_RING)), forward_sem.at[wave])
        wait_for(piece(coeffs, wave, pl.ds(0, n_py - 1)), spread_sem.at[wave])


def transfer(n_py, n_pz, nodal, counts, send_slots, arrival_slots):
    capacity, values = nodal.shape[1:]
    total_slots = n_pz * SLOTS
    elements = total_slots // 2 // BLOCKS
    fourier = jnp.asarray(fourier_table(n_py, elements))
    plane = jnp.asarray(plane_table())
    remote = pl.BlockSpec(memory_space=pltpu.HBM)
    here = functools.partial(pltpu.with_memory_space_constraint, memory_space=pltpu.HBM)
    return pl.pallas_call(
        functools.partial(transfer_kernel, n_py, n_pz),
        out_shape=jax.ShapeDtypeStruct((COMPONENTS, n_py // 8, USED * 16, 128), F32),
        in_specs=[remote] * 6,
        out_specs=pl.BlockSpec(memory_space=pltpu.VMEM),
        scratch_shapes=[
            pltpu.VMEM((COMPONENTS, capacity, values), BF16),
            pltpu.VMEM(counts.shape, jnp.int32),
            pltpu.VMEM(send_slots.shape, jnp.int32),
            pltpu.VMEM(arrival_slots.shape, jnp.int32),
            pltpu.VMEM(fourier.shape, BF16),
            pltpu.VMEM(plane.shape, BF16),
            pltpu.VMEM((total_slots, capacity), BF16),
            pltpu.VMEM((total_slots // 2, total_slots), BF16),
            pltpu.VMEM((COMPONENTS, n_pz, 2, SLOTS, WIDTH), BF16),
            pltpu.VMEM((COMPONENTS, X_RING, 2, SLOTS, WIDTH), BF16),
            pltpu.VMEM((COMPONENTS, n_pz, 2, SLOTS, WIDTH), BF16),
            pltpu.VMEM((NODE * elements, 128), BF16),
            pltpu.VMEM((n_py * TILE, 128), F32),
            pltpu.VMEM((COMPONENTS, n_py, 3, TILE, 128), BF16),
            pltpu.VMEM((COMPONENTS, n_py, 3, TILE, 128), BF16),
            pltpu.SemaphoreType.DMA((8,)),
            *[pltpu.SemaphoreType.DMA((len(WAVES),)) for _ in range(6)],
        ],
        compiler_params=pltpu.CompilerParams(
            collective_id=0, has_side_effects=True, vmem_limit_bytes=40 * 1024 * 1024
        ),
    )(
        here(nodal), counts, here(send_slots), here(arrival_slots), here(fourier), here(plane)
    )


def write_kernel(spectra, out, sem):
    copies = [
        pltpu.make_async_copy(
            spectra.at[c, side], out.at[c, :, pl.ds(side * 128, 128)], sem.at[c, side]
        )
        for c in range(COMPONENTS)
        for side in range(spectra.shape[1])
    ]
    for copy in copies:
        copy.start()
    for copy in copies:
        copy.wait()


def write(spectra):
    sides, rows = spectra.shape[1:3]
    anywhere = pl.BlockSpec(memory_space=pl.ANY)
    return pl.pallas_call(
        write_kernel,
        out_shape=jax.ShapeDtypeStruct((COMPONENTS, rows, sides * 128), F32),
        in_specs=[anywhere],
        out_specs=anywhere,
        scratch_shapes=[pltpu.SemaphoreType.DMA((COMPONENTS, sides))],
        compiler_params=pltpu.CompilerParams(vmem_limit_bytes=40 * 1024 * 1024),
    )(spectra)


def solution(mesh):
    n_py, n_pz = mesh.shape["py"], mesh.shape["pz"]

    def on_device(nodal, element_counts, send_slots, arrival_slots):
        turned = nodal[0].transpose(1, 0, 2)
        spectra = transfer(n_py, n_pz, turned, element_counts, send_slots, arrival_slots)
        return write(spectra).reshape(COMPONENTS, 2, MODES, 16, -1)

    placed = (P("py", "pz", None, None), P("py", "pz"), P("py", "pz"), P("py", "pz"))
    return jax.shard_map(
        on_device,
        mesh=mesh,
        in_specs=placed,
        out_specs=P(None, None, "py", "pz", None),
        check_vma=False,
    )
```

time: 65.4 us -> 64 us (0.979)
  local copies, waits for them, and re-layouts: 2.26 us -> 0 us
  Pallas kernels: 62.3 us -> 63.2 us
    unnamed x1 -> x0, local copies, waits for them, and re-layouts: 2.26 us -> none
    pallas_call x0 -> x1, Pallas kernels: none -> 0.99 us  [write(): pl.pallas_call(write_kernel, out_shape=jax.ShapeDtypeStruct((COMPONENTS,...]
where the time goes in v4:
time: 64 us; the launch traced here: 63.9 us
  Pallas kernels  63.2 us (99%)
  between operations  0.66 us (1%)
    pallas_call x1, Pallas kernels, transfer(): pl.pallas_call(functools.partial(transfer_kernel, n_py, n_pz), out_shape=...  62.2 us

profile of v4, /device:TPU:1, one launch (start us, length us, event | category | flops | bytes accessed | tf_op | source)
XLA Modules:
  0.0 63.9 jit_solution(11141047757509017979)
XLA Ops:
  0.7 62.2 %shard_map.64.spectra = f32[3,2,320,128]{3,2,1,0:T(8,128)S(1)} custom-call(bf16[3,448,512]{2,1,0:T(8,128)(2,1)} %bitcast.4, s32[1,1]{1,0:T(1,128)S(6)} %copy.7.counts, s32[1,448]{1,0:T(1,128)} %send_slots.1, s32[1,512]{1,0:T(1,128)} %arrival_slots.1, bf16[2,256,512]{2,1,0:T(8,128)(2,1)} %constant.4.clone.fourier, bf16[2,512,256]{2,1,0:T(8,128)(2,1)} %constant.5.clone.plane), custom_call_target="tpu_custom_call" | custom-call | tf_op jit(solution)/shard_map/pallas_call | solution.py:369
  62.9 1.0 %shard_map.65 = f32[3,320,256]{2,1,0:T(8,128)} custom-call(f32[3,2,320,128]{3,2,1,0:T(8,128)S(1)} %shard_map.64.spectra), custom_call_target="tpu_custom_call" | custom-call | tf_op jit(solution)/shard_map/pallas_call | solution.py:418

commit v5 on v4

--- a/solution.py
+++ b/solution.py
@@ -197,9 +197,9 @@
 
     def send(wave):
         def far(step, carry):
-            turn = step % (z_ring - 2)
-            side = 1 - (turn + me_y) % 2 * 2
-            send_to(wave, side * (turn // 2 + 1), side * (step // (z_ring - 2)))
+            side = 1 - (step + me_y) % 2 * 2
+            pair = step // 2
+            send_to(wave, side * (pair % (z_ring // 2 - 1) + 1), side * (pair % X_RING))
             return carry
 
         def near(step, carry):
@@ -308,32 +308,32 @@
     pack(0)
     pl.semaphore_wait(barrier, n_pz - 1 + n_py - 1)
     send_opposite(0)
+    send(0)
     loads[5].wait()
     pack(1)
     send_opposite(1)
-    send(0)
+    forward(0)
+    send(1)
     loads[6].wait()
     pack(2)
     send_opposite(2)
     send_opposite(3)
-    forward(0)
-    forward(1)
-    send(1)
     loads[4].wait()
     local = lax.broadcasted_iota(jnp.int32, (place.shape[0], total_slots), 0)
     place[...] = jnp.where(local == arrival_here[...], 1.0, 0.0).astype(BF16)
     loads[7].wait()
+    forward(1)
     receive(0)
-    forward(2)
     send(2)
     transform(0, 0)
     transform(0, 1)
     spread(0)
     receive(1)
+    forward(2)
+    forward(3)
     transform(1, 0)
     transform(1, 1)
     spread(1)
-    forward(3)
     send(3)
     receive(2)
     transform(2, 0)

time: 64 us -> 63.1 us (0.986)
  Pallas kernels: 63.2 us -> 62.3 us
    pallas_call x1, Pallas kernels: 62.2 us -> 61.3 us  [transfer(): pl.pallas_call(functools.partial(transfer_kernel, n_py, n_pz), out_shape=...]
where the time goes in v5:
time: 63.1 us; the launch traced here: 63 us
  Pallas kernels  62.3 us (99%)
  between operations  0.66 us (1%)
    pallas_call x1, Pallas kernels, transfer(): pl.pallas_call(functools.partial(transfer_kernel, n_py, n_pz), out_shape=...  61.3 us

profile of v5, /device:TPU:1, one launch (start us, length us, event | category | flops | bytes accessed | tf_op | source)
XLA Modules:
  0.0 63.0 jit_solution(6586132303872820306)
XLA Ops:
  0.7 61.3 %shard_map.64.spectra = f32[3,2,320,128]{3,2,1,0:T(8,128)S(1)} custom-call(bf16[3,448,512]{2,1,0:T(8,128)(2,1)} %bitcast.4, s32[1,1]{1,0:T(1,128)S(6)} %copy.7.counts, s32[1,448]{1,0:T(1,128)} %send_slots.1, s32[1,512]{1,0:T(1,128)} %arrival_slots.1, bf16[2,256,512]{2,1,0:T(8,128)(2,1)} %constant.4.clone.fourier, bf16[2,512,256]{2,1,0:T(8,128)(2,1)} %constant.5.clone.plane), custom_call_target="tpu_custom_call" | custom-call | tf_op jit(solution)/shard_map/pallas_call | solution.py:369
  62.0 1.0 %shard_map.65 = f32[3,320,256]{2,1,0:T(8,128)} custom-call(f32[3,2,320,128]{3,2,1,0:T(8,128)S(1)} %shard_map.64.spectra), custom_call_target="tpu_custom_call" | custom-call | tf_op jit(solution)/shard_map/pallas_call | solution.py:418

commit v6 on v5

--- a/solution.py
+++ b/solution.py
@@ -22,8 +22,9 @@
 TILE = 16
 LEFT = USED - TILE
 GROUP = 8
-WAVES = ((0, 0, 2), (1, 0, 2), (2, 0, 1), (2, 1, 1))
-PARTS = ((0, 0, 3), (1, 0, 3), (2, 0, 1), (2, 1, 2))
+WAVES = ((0, 0, 2, 0, 256), (1, 0, 2, 0, 256), (2, 0, 1, 0, 256), (2, 1, 1, 0, 128), (2, 1, 1, 128, 128))
+PARTS = ((0, 0, 3), (1, 0, 3), (2, 0, 2), (2, 2, 1), (2, 3, 1))
+LAST = COMPONENTS - 1
 WIDTH = NODE**3 // 2
 BF16 = jnp.bfloat16
 F32 = jnp.float32
@@ -75,8 +76,11 @@
 def plane_table():
     lagrange = vandermonde(NODE)
     table = np.einsum("fu,gv,hw->uvhwfg", lagrange, lagrange, np.eye(NODE))
-    table = table.reshape(NODE**3, NODE, 2, NODE // 2, NODE).transpose(2, 0, 1, 3, 4)
-    return table.reshape(2, NODE**3, NODE**3 // 2).astype(ml_dtypes.bfloat16)
+    halves = table.reshape(NODE**3, NODE, 2, NODE // 2, NODE).transpose(2, 0, 1, 3, 4)
+    quarters = halves[1].reshape(NODE**3, NODE, 2, NODE // 4, NODE).transpose(0, 2, 1, 3, 4)
+    tables = [halves[0], halves[1], quarters]
+    tables = [table.reshape(NODE**3, NODE**3 // 2) for table in tables]
+    return np.stack(tables).astype(ml_dtypes.bfloat16)
 
 
 def exchange(tiles, index_bit, lane_bit, width):
@@ -148,7 +152,8 @@
 
     def pack(c):
         for half in range(2):
-            turned = jnp.dot(nodes[c], plane_here[half], preferred_element_type=F32).astype(BF16)
+            table = plane_here[2 if c == LAST and half == 1 else half]
+            turned = jnp.dot(nodes[c], table, preferred_element_type=F32).astype(BF16)
             packed = jnp.dot(pick[...], turned, preferred_element_type=F32).astype(BF16)
             outgoing[c, :, half] = packed.reshape(n_pz, SLOTS, WIDTH)
 
@@ -157,8 +162,8 @@
         return peer_plane * X_RING + (my_column + column_step + X_RING) % X_RING
 
     def block(ref, wave, device):
-        c, first, number = WAVES[wave]
-        return ref.at[c, device, pl.ds(first, number)]
+        c, first, number, lane, lanes = WAVES[wave]
+        return ref.at[c, device, pl.ds(first, number), :, pl.ds(lane, lanes)]
 
     def piece(ref, wave, device):
         c, first, number = PARTS[wave]
@@ -208,9 +213,10 @@
 
         lax.fori_loop(1, X_RING, near, 0)
         lax.fori_loop(0, (z_ring - 2) * X_RING, far, 0)
-        c, first, number = WAVES[wave]
+        c, first, number, lane, lanes = WAVES[wave]
+        here = pl.ds(lane, lanes)
         for half in range(first, first + number):
-            arrived[c, me_z, half] = outgoing[c, me_z, half]
+            arrived[c, me_z, half, :, here] = outgoing[c, me_z, half, :, here]
 
     def forward(wave):
         wait_for(block(relayed, wave, pl.ds(0, X_RING)), relay_sem.at[wave])
@@ -253,11 +259,35 @@
             result = jnp.dot(fourier_here[0, here], stacked[...], preferred_element_type=F32)
             coeffs[c, members, half] = result.astype(BF16).reshape(GROUP, TILE, 128)
             rest = jnp.dot(fourier_here[1, here], stacked[...], preferred_element_type=F32)
-            if half == 0:
+            if c == LAST:
+                coeffs[c, members, 1] = rest.astype(BF16).reshape(GROUP, TILE, 128)
+            elif half == 0:
                 leftover[here] = rest
             else:
                 both = leftover[here] + pltpu.roll(rest, LEFT, 0)
                 coeffs[c, members, 2] = both.astype(BF16).reshape(GROUP, TILE, 128)
+            return carry
+
+        lax.fori_loop(0, groups, group_step, 0)
+
+    def transform_quarter(quarter_at):
+        slots = arrived[LAST, :, 1, :, pl.ds(quarter_at * 128, 128)].reshape(total_slots, 128)
+        placed = jnp.dot(place[...], slots, preferred_element_type=F32)
+        tiles = [placed[at * elements : (at + 1) * elements] for at in range(BLOCKS)]
+        tiles = exchange(exchange(tiles, 1, 1, 16), 2, 2, 16)
+        for at, tile in enumerate(tiles):
+            stacked[pl.ds(at * elements, elements), :] = tile.astype(BF16)
+            stacked[pl.ds((4 + at) * elements, elements), :] = pltpu.roll(tile, 64, 1).astype(BF16)
+
+        def group_step(step, carry):
+            here = pl.ds(pl.multiple_of(step * rows, rows), rows)
+            result = jnp.dot(fourier_here[0, here], stacked[...], preferred_element_type=F32)
+            rest = jnp.dot(fourier_here[1, here], stacked[...], preferred_element_type=F32)
+            lane = lax.broadcasted_iota(jnp.int32, result.shape, 1)
+            both = jnp.where(lane < 64, result, pltpu.roll(rest, 64, 1))
+            coeffs[LAST, pl.ds(step * GROUP, GROUP), 2 + quarter_at] = both.astype(BF16).reshape(
+                GROUP, TILE, 128
+            )
             return carry
 
         lax.fori_loop(0, groups, group_step, 0)
@@ -285,20 +315,40 @@
         wait_for(piece(received, wave, pl.ds(0, n_py - 1)), receive_sem.at[wave])
 
     def put_in_order(c, part):
+        rest = part == (1 if c == LAST else 2)
+
         def side_step(side, carry):
             tiles = [received[c, side * 8 + band, part].astype(F32) for band in range(8)]
-            if part == 2:
+            if rest:
                 tiles = [tile[: 2 * LEFT] for tile in tiles]
             for index_bit, lane_bit in ((4, 8), (2, 4), (1, 2), (2, 1)):
                 tiles = exchange(tiles, index_bit, lane_bit, 8)
             for at in range(8):
                 z = at // 4 * 8 + at % 2 * 2 + at // 2 % 2
-                if part == 2:
-                    for half in range(2):
+                if rest:
+                    for half in range(1 if c == LAST else 2):
                         here = pl.ds(TILE * 16 + half * 4 + z, LEFT, stride=16)
                         out[c, side, here, :] = tiles[at][half * LEFT : (half + 1) * LEFT]
                 else:
                     out[c, side, pl.ds(part * 4 + z, TILE, stride=16), :] = tiles[at]
+            return carry
+
+        lax.fori_loop(0, n_py // 8, side_step, 0)
+
+    def put_quarter_in_order(quarter_at):
+        def side_step(side, carry):
+            tiles = [
+                received[LAST, side * 8 + band, 2 + quarter_at].astype(F32) for band in range(8)
+            ]
+            for index_bit, lane_bit in ((4, 8), (2, 4), (1, 2), (1, 1)):
+                tiles = exchange(tiles, index_bit, lane_bit, 8)
+            for at in range(8):
+                z = 4 + quarter_at * 2 + at // 2 % 2 * 8 + at % 2
+                if at < 4:
+                    out[LAST, side, pl.ds(z, TILE, stride=16), :] = tiles[at]
+                else:
+                    here = pl.ds(TILE * 16 + z, LEFT, stride=16)
+                    out[LAST, side, here, :] = tiles[at][:LEFT]
             return carry
 
         lax.fori_loop(0, n_py // 8, side_step, 0)
@@ -318,6 +368,7 @@
     pack(2)
     send_opposite(2)
     send_opposite(3)
+    send_opposite(4)
     loads[4].wait()
     local = lax.broadcasted_iota(jnp.int32, (place.shape[0], total_slots), 0)
     place[...] = jnp.where(local == arrival_here[...], 1.0, 0.0).astype(BF16)
@@ -331,10 +382,12 @@
     receive(1)
     forward(2)
     forward(3)
+    forward(4)
     transform(1, 0)
     transform(1, 1)
     spread(1)
     send(3)
+    send(4)
     receive(2)
     transform(2, 0)
     spread(2)
@@ -342,16 +395,21 @@
     for part in range(3):
         put_in_order(0, part)
     receive(3)
-    transform(2, 1)
+    transform_quarter(0)
     spread(3)
+    receive(4)
+    transform_quarter(1)
+    spread(4)
     gather(1)
     for part in range(3):
         put_in_order(1, part)
     gather(2)
     put_in_order(2, 0)
+    put_in_order(2, 1)
     gather(3)
-    put_in_order(2, 1)
-    put_in_order(2, 2)
+    put_quarter_in_order(0)
+    gather(4)
+    put_quarter_in_order(1)
     for wave in range(len(WAVES)):
         wait_for(block(outgoing, wave, pl.ds(0, n_pz - 1)), send_sem.at[wave])
         wait_for(block(relayed, wave, pl.ds(0, X_RING)), forward_sem.at[wave])
@@ -385,8 +443,8 @@
             pltpu.VMEM((COMPONENTS, n_pz, 2, SLOTS, WIDTH), BF16),
             pltpu.VMEM((NODE * elements, 128), BF16),
             pltpu.VMEM((n_py * TILE, 128), F32),
-            pltpu.VMEM((COMPONENTS, n_py, 3, TILE, 128), BF16),
-            pltpu.VMEM((COMPONENTS, n_py, 3, TILE, 128), BF16),
+            pltpu.VMEM((COMPONENTS, n_py, 4, TILE, 128), BF16),
+            pltpu.VMEM((COMPONENTS, n_py, 4, TILE, 128), BF16),
             pltpu.SemaphoreType.DMA((8,)),
             *[pltpu.SemaphoreType.DMA((len(WAVES),)) for _ in range(6)],
         ],

time: 63.1 us -> 63.1 us (level)
  no operation moved by 1% of the time
where the time goes in v6:
time: 63.1 us; the launch traced here: 63 us
  Pallas kernels  62.3 us (99%)
  between operations  0.66 us (1%)
    pallas_call x1, Pallas kernels, transfer(): pl.pallas_call(functools.partial(transfer_kernel, n_py, n_pz), out_shape=...  61.3 us

profile of v6, /device:TPU:1, one launch (start us, length us, event | category | flops | bytes accessed | tf_op | source)
XLA Modules:
  0.0 63.0 jit_solution(14654744286161283548)
XLA Ops:
  0.7 61.3 %shard_map.64.spectra = f32[3,2,320,128]{3,2,1,0:T(8,128)S(1)} custom-call(bf16[3,448,512]{2,1,0:T(8,128)(2,1)} %bitcast.4, s32[1,1]{1,0:T(1,128)S(6)} %copy.7.counts, s32[1,448]{1,0:T(1,128)} %send_slots.1, s32[1,512]{1,0:T(1,128)} %arrival_slots.1, bf16[2,256,512]{2,1,0:T(8,128)(2,1)} %constant.4.clone.fourier, bf16[3,512,256]{2,1,0:T(8,128)(2,1)} %constant.5.clone.plane), custom_call_target="tpu_custom_call" | custom-call | tf_op jit(solution)/shard_map/pallas_call | solution.py:427
  62.0 1.0 %shard_map.65 = f32[3,320,256]{2,1,0:T(8,128)} custom-call(f32[3,2,320,128]{3,2,1,0:T(8,128)S(1)} %shard_map.64.spectra), custom_call_target="tpu_custom_call" | custom-call | tf_op jit(solution)/shard_map/pallas_call | solution.py:476

commit v7 on v5

--- a/solution.py
+++ b/solution.py
@@ -21,7 +21,6 @@
 USED = 2 * MODES
 TILE = 16
 LEFT = USED - TILE
-GROUP = 8
 WAVES = ((0, 0, 2), (1, 0, 2), (2, 0, 1), (2, 1, 1))
 PARTS = ((0, 0, 3), (1, 0, 3), (2, 0, 1), (2, 1, 2))
 WIDTH = NODE**3 // 2
@@ -69,7 +68,7 @@
     table = np.zeros((2, bands, TILE, NODE, elements))
     table[0] = nodes[:, :TILE]
     table[1, :, :LEFT] = nodes[:, TILE:]
-    return table.reshape(2, bands * TILE, NODE * elements).astype(ml_dtypes.bfloat16)
+    return table.reshape(2 * bands * TILE, NODE * elements).astype(ml_dtypes.bfloat16)
 
 
 def plane_table():
@@ -179,9 +178,10 @@
         ).start()
 
     quarter = z_ring // 4
+    first_side = 1 - me_y % 2 * 2
 
     def send_opposite(wave):
-        def opposite(step, carry):
+        for step in range(X_RING):
             way = (1 - step % 2 * 2) * quarter
             pltpu.make_async_remote_copy(
                 src_ref=block(outgoing, wave, peer_at(2 * quarter, step)),
@@ -191,31 +191,29 @@
                 device_id={"pz": peer_at(way, step)},
                 device_id_type=MESH,
             ).start()
-            return carry
-
-        lax.fori_loop(0, X_RING, opposite, 0)
-
-    def send(wave):
-        def far(step, carry):
-            side = 1 - (step + me_y) % 2 * 2
-            pair = step // 2
-            send_to(wave, side * (pair % (z_ring // 2 - 1) + 1), side * (pair % X_RING))
-            return carry
-
-        def near(step, carry):
-            send_to(wave, 0, step)
-            return carry
-
-        lax.fori_loop(1, X_RING, near, 0)
-        lax.fori_loop(0, (z_ring - 2) * X_RING, far, 0)
+
+    pairs_far = [(p % (z_ring // 2 - 1) + 1, p % X_RING) for p in range((z_ring // 2 - 1) * X_RING)]
+
+    def send_far(wave, chosen):
+        for distance, column in chosen:
+            for side in (first_side, -first_side):
+                send_to(wave, side * distance, side * column)
+
+    def send_near(wave):
+        for column in range(1, X_RING):
+            send_to(wave, 0, column)
         c, first, number = WAVES[wave]
         for half in range(first, first + number):
             arrived[c, me_z, half] = outgoing[c, me_z, half]
 
+    def send(wave):
+        send_near(wave)
+        send_far(wave, pairs_far)
+
     def forward(wave):
         wait_for(block(relayed, wave, pl.ds(0, X_RING)), relay_sem.at[wave])
 
-        def onward(step, carry):
+        for step in range(X_RING):
             way = (1 - step % 2 * 2) * quarter
             pltpu.make_async_remote_copy(
                 src_ref=block(relayed, wave, step),
@@ -225,15 +223,9 @@
                 device_id={"pz": peer_at(way, 0)},
                 device_id_type=MESH,
             ).start()
-            return carry
-
-        lax.fori_loop(0, X_RING, onward, 0)
 
     def receive(wave):
         wait_for(block(arrived, wave, pl.ds(0, n_pz - 1)), arrive_sem.at[wave])
-
-    rows = GROUP * TILE
-    groups = n_py // GROUP
 
     def transform(c, half):
         slots = arrived[c, :, half].reshape(total_slots, WIDTH)
@@ -247,27 +239,21 @@
             for at, tile in enumerate(tiles):
                 stacked[pl.ds((quad * 4 + at) * elements, elements), :] = tile.astype(BF16)
 
-        def group_step(step, carry):
-            here = pl.ds(pl.multiple_of(step * rows, rows), rows)
-            members = pl.ds(step * GROUP, GROUP)
-            result = jnp.dot(fourier_here[0, here], stacked[...], preferred_element_type=F32)
-            coeffs[c, members, half] = result.astype(BF16).reshape(GROUP, TILE, 128)
-            rest = jnp.dot(fourier_here[1, here], stacked[...], preferred_element_type=F32)
-            if half == 0:
-                leftover[here] = rest
-            else:
-                both = leftover[here] + pltpu.roll(rest, LEFT, 0)
-                coeffs[c, members, 2] = both.astype(BF16).reshape(GROUP, TILE, 128)
-            return carry
-
-        lax.fori_loop(0, groups, group_step, 0)
+        result = jnp.dot(fourier_here[...], stacked[...], preferred_element_type=F32)
+        main, rest = result[: n_py * TILE], result[n_py * TILE :]
+        coeffs[c, :, half] = main.astype(BF16).reshape(n_py, TILE, 128)
+        if half == 0:
+            leftover[...] = rest
+        else:
+            both = leftover[...] + pltpu.roll(rest, LEFT, 0)
+            coeffs[c, :, 2] = both.astype(BF16).reshape(n_py, TILE, 128)
 
     def spread(wave):
         c, first, number = PARTS[wave]
         for part in range(first, first + number):
             received[c, me_y, part] = coeffs[c, me_y, part]
 
-        def spread_to(step, carry):
+        for step in range(1, n_py):
             peer = (me_y + (step + 1) // 2 * (1 - step % 2 * 2) + n_py) % n_py
             pltpu.make_async_remote_copy(
                 src_ref=piece(coeffs, wave, peer),
@@ -277,9 +263,6 @@
                 device_id={"py": peer},
                 device_id_type=MESH,
             ).start()
-            return carry
-
-        lax.fori_loop(1, n_py, spread_to, 0)
 
     def gather(wave):
         wait_for(piece(received, wave, pl.ds(0, n_py - 1)), receive_sem.at[wave])
@@ -332,9 +315,11 @@
     forward(2)
     forward(3)
     transform(1, 0)
+    send_near(3)
+    send_far(3, pairs_far[: len(pairs_far) // 2])
     transform(1, 1)
     spread(1)
-    send(3)
+    send_far(3, pairs_far[len(pairs_far) // 2 :])
     receive(2)
     transform(2, 0)
     spread(2)

time: 63.1 us -> 63.3 us (level)
  no operation moved by 1% of the time
where the time goes in v7:
time: 63.3 us; the launch traced here: 63.1 us
  Pallas kernels  62.5 us (99%)
  between operations  0.66 us (1%)
    pallas_call x1, Pallas kernels, transfer(): pl.pallas_call(functools.partial(transfer_kernel, n_py, n_pz), out_shape=...  61.5 us

profile of v7, /device:TPU:1, one launch (start us, length us, event | category | flops | bytes accessed | tf_op | source)
XLA Modules:
  0.0 63.1 jit_solution(7539192410186324293)
XLA Ops:
  0.7 61.5 %shard_map.64.spectra = f32[3,2,320,128]{3,2,1,0:T(8,128)S(1)} custom-call(bf16[3,448,512]{2,1,0:T(8,128)(2,1)} %bitcast.4, s32[1,1]{1,0:T(1,128)S(6)} %copy.7.counts, s32[1,448]{1,0:T(1,128)} %send_slots.1, s32[1,512]{1,0:T(1,128)} %arrival_slots.1, bf16[512,512]{1,0:T(8,128)(2,1)} %constant.4.clone.fourier, bf16[2,512,256]{2,1,0:T(8,128)(2,1)} %constant.5.clone.plane), custom_call_target="tpu_custom_call" | custom-call | tf_op jit(solution)/shard_map/pallas_call | solution.py:354
  62.1 1.0 %shard_map.65 = f32[3,320,256]{2,1,0:T(8,128)} custom-call(f32[3,2,320,128]{3,2,1,0:T(8,128)S(1)} %shard_map.64.spectra), custom_call_target="tpu_custom_call" | custom-call | tf_op jit(solution)/shard_map/pallas_call | solution.py:403

commit v8 on v7

--- a/solution.py
+++ b/solution.py
@@ -94,8 +94,8 @@
 def transfer_kernel(
     n_py, n_pz, nodal, counts, send_slots, arrival_slots, fourier, plane, out,
     nodes, counts_here, send_here, arrival_here, fourier_here, plane_here, pick, place,
-    outgoing, relayed, arrived, stacked, leftover, coeffs, received,
-    load_sem, send_sem, relay_sem, forward_sem, arrive_sem, spread_sem, receive_sem,
+    outgoing, arrived, stacked, leftover, coeffs, received,
+    load_sem, send_sem, arrive_sem, spread_sem, receive_sem,
 ):
     me_y = lax.axis_index("py")
     me_z = lax.axis_index("pz")
@@ -177,27 +177,17 @@
             device_id_type=MESH,
         ).start()
 
-    quarter = z_ring // 4
     first_side = 1 - me_y % 2 * 2
-
-    def send_opposite(wave):
-        for step in range(X_RING):
-            way = (1 - step % 2 * 2) * quarter
-            pltpu.make_async_remote_copy(
-                src_ref=block(outgoing, wave, peer_at(2 * quarter, step)),
-                dst_ref=block(relayed, wave, step),
-                send_sem=send_sem.at[wave],
-                recv_sem=relay_sem.at[wave],
-                device_id={"pz": peer_at(way, step)},
-                device_id_type=MESH,
-            ).start()
-
-    pairs_far = [(p % (z_ring // 2 - 1) + 1, p % X_RING) for p in range((z_ring // 2 - 1) * X_RING)]
+    half_ring = z_ring // 2
+    far = []
+    for p in range((half_ring - 1) * X_RING):
+        far += [(side, p % (half_ring - 1) + 1, p % X_RING) for side in (1, -1)]
+        if p % (half_ring - 1) == half_ring - 2:
+            far.append((1, half_ring, p // (half_ring - 1)))
 
     def send_far(wave, chosen):
-        for distance, column in chosen:
-            for side in (first_side, -first_side):
-                send_to(wave, side * distance, side * column)
+        for side, distance, column in chosen:
+            send_to(wave, first_side * side * distance, first_side * side * column)
 
     def send_near(wave):
         for column in range(1, X_RING):
@@ -208,21 +198,7 @@
 
     def send(wave):
         send_near(wave)
-        send_far(wave, pairs_far)
-
-    def forward(wave):
-        wait_for(block(relayed, wave, pl.ds(0, X_RING)), relay_sem.at[wave])
-
-        for step in range(X_RING):
-            way = (1 - step % 2 * 2) * quarter
-            pltpu.make_async_remote_copy(
-                src_ref=block(relayed, wave, step),
-                dst_ref=block(arrived, wave, peer_at(-way, -step)),
-                send_sem=forward_sem.at[wave],
-                recv_sem=arrive_sem.at[wave],
-                device_id={"pz": peer_at(way, 0)},
-                device_id_type=MESH,
-            ).start()
+        send_far(wave, far)
 
     def receive(wave):
         wait_for(block(arrived, wave, pl.ds(0, n_pz - 1)), arrive_sem.at[wave])
@@ -290,36 +266,28 @@
     loads[3].wait()
     pack(0)
     pl.semaphore_wait(barrier, n_pz - 1 + n_py - 1)
-    send_opposite(0)
     send(0)
     loads[5].wait()
     pack(1)
-    send_opposite(1)
-    forward(0)
     send(1)
     loads[6].wait()
     pack(2)
-    send_opposite(2)
-    send_opposite(3)
     loads[4].wait()
     local = lax.broadcasted_iota(jnp.int32, (place.shape[0], total_slots), 0)
     place[...] = jnp.where(local == arrival_here[...], 1.0, 0.0).astype(BF16)
     loads[7].wait()
-    forward(1)
     receive(0)
     send(2)
     transform(0, 0)
     transform(0, 1)
     spread(0)
     receive(1)
-    forward(2)
-    forward(3)
     transform(1, 0)
     send_near(3)
-    send_far(3, pairs_far[: len(pairs_far) // 2])
+    send_far(3, far[: len(far) // 2])
     transform(1, 1)
     spread(1)
-    send_far(3, pairs_far[len(pairs_far) // 2 :])
+    send_far(3, far[len(far) // 2 :])
     receive(2)
     transform(2, 0)
     spread(2)
@@ -339,7 +307,6 @@
     put_in_order(2, 2)
     for wave in range(len(WAVES)):
         wait_for(block(outgoing, wave, pl.ds(0, n_pz - 1)), send_sem.at[wave])
-        wait_for(block(relayed, wave, pl.ds(0, X_RING)), forward_sem.at[wave])
         wait_for(piece(coeffs, wave, pl.ds(0, n_py - 1)), spread_sem.at[wave])
 
 
@@ -366,14 +333,13 @@
             pltpu.VMEM((total_slots, capacity), BF16),
             pltpu.VMEM((total_slots // 2, total_slots), BF16),
             pltpu.VMEM((COMPONENTS, n_pz, 2, SLOTS, WIDTH), BF16),
-            pltpu.VMEM((COMPONENTS, X_RING, 2, SLOTS, WIDTH), BF16),
             pltpu.VMEM((COMPONENTS, n_pz, 2, SLOTS, WIDTH), BF16),
             pltpu.VMEM((NODE * elements, 128), BF16),
             pltpu.VMEM((n_py * TILE, 128), F32),
             pltpu.VMEM((COMPONENTS, n_py, 3, TILE, 128), BF16),
             pltpu.VMEM((COMPONENTS, n_py, 3, TILE, 128), BF16),
             pltpu.SemaphoreType.DMA((8,)),
-            *[pltpu.SemaphoreType.DMA((len(WAVES),)) for _ in range(6)],
+            *[pltpu.SemaphoreType.DMA((len(WAVES),)) for _ in range(4)],
         ],
         compiler_params=pltpu.CompilerParams(
             collective_id=0, has_side_effects=True, vmem_limit_bytes=40 * 1024 * 1024

time: 63.3 us -> 63.4 us (level)
  no operation moved by 1% of the time
where the time goes in v8:
time: 63.4 us; the launch traced here: 63.2 us
  Pallas kernels  62.6 us (99%)
  between operations  0.66 us (1%)
    pallas_call x1, Pallas kernels, transfer(): pl.pallas_call(functools.partial(transfer_kernel, n_py, n_pz), out_shape=...  61.6 us

profile of v8, /device:TPU:1, one launch (start us, length us, event | category | flops | bytes accessed | tf_op | source)
XLA Modules:
  0.0 63.2 jit_solution(9364423448229011749)
XLA Ops:
  0.7 61.6 %shard_map.64.spectra = f32[3,2,320,128]{3,2,1,0:T(8,128)S(1)} custom-call(bf16[3,448,512]{2,1,0:T(8,128)(2,1)} %bitcast.4, s32[1,1]{1,0:T(1,128)S(6)} %copy.7.counts, s32[1,448]{1,0:T(1,128)} %send_slots.1, s32[1,512]{1,0:T(1,128)} %arrival_slots.1, bf16[512,512]{1,0:T(8,128)(2,1)} %constant.4.clone.fourier, bf16[2,512,256]{2,1,0:T(8,128)(2,1)} %constant.5.clone.plane), custom_call_target="tpu_custom_call" | custom-call | tf_op jit(solution)/shard_map/pallas_call | solution.py:321
  62.2 1.0 %shard_map.65 = f32[3,320,256]{2,1,0:T(8,128)} custom-call(f32[3,2,320,128]{3,2,1,0:T(8,128)S(1)} %shard_map.64.spectra), custom_call_target="tpu_custom_call" | custom-call | tf_op jit(solution)/shard_map/pallas_call | solution.py:369

commit v9 on v5

--- a/solution.py
+++ b/solution.py
@@ -134,7 +134,7 @@
         pltpu.make_async_copy(source, here, load_sem.at[at])
         for at, (source, here) in enumerate(pairs)
     ]
-    for load in loads:
+    for load in loads[:4]:
         load.start()
     lax.fori_loop(1, n_pz, greet_z, 0)
     lax.fori_loop(1, n_py, greet_y, 0)
@@ -146,8 +146,8 @@
     row = lax.broadcasted_iota(jnp.int32, (total_slots, capacity), 0)
     pick[...] = jnp.where(row == target, 1.0, 0.0).astype(BF16)
 
-    def pack(c):
-        for half in range(2):
+    def pack(c, halves=(0, 1)):
+        for half in halves:
             turned = jnp.dot(nodes[c], plane_here[half], preferred_element_type=F32).astype(BF16)
             packed = jnp.dot(pick[...], turned, preferred_element_type=F32).astype(BF16)
             outgoing[c, :, half] = packed.reshape(n_pz, SLOTS, WIDTH)
@@ -156,8 +156,9 @@
         peer_plane = (my_plane + plane_step + z_ring) % z_ring
         return peer_plane * X_RING + (my_column + column_step + X_RING) % X_RING
 
-    def block(ref, wave, device):
+    def block(ref, wave, device, span=None):
         c, first, number = WAVES[wave]
+        first, number = span or (first, number)
         return ref.at[c, device, pl.ds(first, number)]
 
     def piece(ref, wave, device):
@@ -167,11 +168,11 @@
     def wait_for(part, sem):
         pltpu.make_async_copy(part, part, sem).wait()
 
-    def send_to(wave, plane_step, column_step):
+    def send_to(wave, plane_step, column_step, span):
         peer = peer_at(plane_step, column_step)
         pltpu.make_async_remote_copy(
-            src_ref=block(outgoing, wave, peer),
-            dst_ref=block(arrived, wave, me_z),
+            src_ref=block(outgoing, wave, peer, span),
+            dst_ref=block(arrived, wave, me_z, span),
             send_sem=send_sem.at[wave],
             recv_sem=arrive_sem.at[wave],
             device_id={"pz": peer},
@@ -180,12 +181,12 @@
 
     quarter = z_ring // 4
 
-    def send_opposite(wave):
+    def send_opposite(wave, span=None):
         def opposite(step, carry):
             way = (1 - step % 2 * 2) * quarter
             pltpu.make_async_remote_copy(
-                src_ref=block(outgoing, wave, peer_at(2 * quarter, step)),
-                dst_ref=block(relayed, wave, step),
+                src_ref=block(outgoing, wave, peer_at(2 * quarter, step), span),
+                dst_ref=block(relayed, wave, step, span),
                 send_sem=send_sem.at[wave],
                 recv_sem=relay_sem.at[wave],
                 device_id={"pz": peer_at(way, step)},
@@ -195,20 +196,21 @@
 
         lax.fori_loop(0, X_RING, opposite, 0)
 
-    def send(wave):
+    def send(wave, span=None):
         def far(step, carry):
             side = 1 - (step + me_y) % 2 * 2
             pair = step // 2
-            send_to(wave, side * (pair % (z_ring // 2 - 1) + 1), side * (pair % X_RING))
+            send_to(wave, side * (pair % (z_ring // 2 - 1) + 1), side * (pair % X_RING), span)
             return carry
 
         def near(step, carry):
-            send_to(wave, 0, step)
+            send_to(wave, 0, step, span)
             return carry
 
         lax.fori_loop(1, X_RING, near, 0)
         lax.fori_loop(0, (z_ring - 2) * X_RING, far, 0)
         c, first, number = WAVES[wave]
+        first, number = span or (first, number)
         for half in range(first, first + number):
             arrived[c, me_z, half] = outgoing[c, me_z, half]
 
@@ -305,10 +307,15 @@
 
     loads[2].wait()
     loads[3].wait()
-    pack(0)
+    pack(0, (0,))
     pl.semaphore_wait(barrier, n_pz - 1 + n_py - 1)
-    send_opposite(0)
-    send(0)
+    send_opposite(0, (0, 1))
+    send(0, (0, 1))
+    for load in loads[4:]:
+        load.start()
+    pack(0, (1,))
+    send_opposite(0, (1, 1))
+    send(0, (1, 1))
     loads[5].wait()
     pack(1)
     send_opposite(1)

time: 63.1 us -> 63.7 us (level)
  no operation moved by 1% of the time
where the time goes in v9:
time: 63.7 us; the launch traced here: 63.5 us
  Pallas kernels  62.8 us (99%)
  between operations  0.66 us (1%)
    pallas_call x1, Pallas kernels, transfer(): pl.pallas_call(functools.partial(transfer_kernel, n_py, n_pz), out_shape=...  61.9 us

profile of v9, /device:TPU:1, one launch (start us, length us, event | category | flops | bytes accessed | tf_op | source)
XLA Modules:
  0.0 63.5 jit_solution(2366279690641617917)
XLA Ops:
  0.7 61.9 %shard_map.64.spectra = f32[3,2,320,128]{3,2,1,0:T(8,128)S(1)} custom-call(bf16[3,448,512]{2,1,0:T(8,128)(2,1)} %bitcast.4, s32[1,1]{1,0:T(1,128)S(6)} %copy.7.counts, s32[1,448]{1,0:T(1,128)} %send_slots.1, s32[1,512]{1,0:T(1,128)} %arrival_slots.1, bf16[2,256,512]{2,1,0:T(8,128)(2,1)} %constant.4.clone.fourier, bf16[2,512,256]{2,1,0:T(8,128)(2,1)} %constant.5.clone.plane), custom_call_target="tpu_custom_call" | custom-call | tf_op jit(solution)/shard_map/pallas_call | solution.py:376
  62.5 1.0 %shard_map.65 = f32[3,320,256]{2,1,0:T(8,128)} custom-call(f32[3,2,320,128]{3,2,1,0:T(8,128)S(1)} %shard_map.64.spectra), custom_call_target="tpu_custom_call" | custom-call | tf_op jit(solution)/shard_map/pallas_call | solution.py:425
